TPU v7x, 256 devices: a whole 4x4x8 slice. The times are simulated.
256 devices in a mesh: grp: 8 (over x, core), tile: 32 (over z, y).
Axes of the slice: x: 4, y: 4, z: 8, core: 2. Of those that a mesh axis runs over, the one named last changes fastest.
Arguments:
- features: bfloat16 [65536, 1024], P(('grp', 'tile'))
- projection: bfloat16 [1024, 768], replicated, may hold values from -0.1875 to 0.1875
- pooled_grad: bfloat16 [96, 768, 768], P('grp', 'tile'), may hold values from -96 to 96
- slide_counts: int32 [96], P('grp'), may hold values from 321 to 2176, as said below
- slide_offsets: int32 [96], P('grp'), may hold values from 0 to 7808, as said below
Outputs:
- feature_grad: bfloat16 [65536, 1024], P(('grp', 'tile'))
- projection_grad: float32 [1024, 768], replicated
Inputs may be any that keep to these rules, and one draw needn't show every extreme that they name: Within each group the slides lie end to end from row 0 and fill all 8192 rows in order; each slide spans a multiple of 128 rows, at least 384, and the last slide of each group exactly 384; slide_offsets gives each slide's first row within its group. A slide's first slide_counts rows are tiles, the rest of its span, fewer than 64 rows, is padding; a largest slide of each group, never the last, has no padding.
All inputs are finite; a program needn't handle non-finite values.
Results may differ from a plain program's by a relative error of at most 0.011.
Values may be sent and summed in bfloat16 or wider, within the bound.
No kernel may reach another device: no remote copies, remote signals or barrier semaphores. Data moves between devices by JAX's collectives and lax.ppermute only.
A program may use at most 256 MiB of HBM per device.

v0:
```python
import functools

import jax
import jax.numpy as jnp
from jax import lax
from jax.experimental import pallas as pl
from jax.experimental.pallas import tpu as pltpu
from jax.sharding import PartitionSpec as P

BF = jnp.bfloat16
F32 = jnp.float32
ROWS = 256
PLANE = 4 * ROWS
DIN = 1024
D = 768
CHUNK = 256
CHUNKS = D // CHUNK
PAIRS = [(i, j) for i in range(6) for j in range(i + 1)]
STRIP = 32
TAIL = len(PAIRS) * STRIP
MESSAGE = TAIL + 16
PIECES = ((0, 0, ROWS), (1, 0, ROWS), (2, 0, ROWS // 2), (2, ROWS // 2, ROWS // 2), (3, 0, ROWS))
VMEM = pl.BlockSpec(memory_space=pltpu.VMEM)
SMEM = pl.BlockSpec(memory_space=pltpu.SMEM)

BASE, OWN, FIRST, LAST, QUARTER, GRAD, EXTRA, END, ALONE, PLACE = 0, 4, 6, 8, 10, 11, 12, 13, 14, 15
COUNT, SCALARS = 20, 21

WORK = 5 * 10**9
CORE_PAIRS = [(i, i ^ 1) for i in range(8)]


def x_shift(step):
    return [(x * 2 + c, (x + step) % 4 * 2 + c) for x in range(4) for c in range(2)]


def y_shift(step):
    return [(z * 4 + y, z * 4 + (y + step) % 4) for z in range(8) for y in range(4)]


def z_shift(step):
    return [(z * 4 + y, (z + step) % 8 * 4 + y) for z in range(8) for y in range(4)]


def y_to_ends(step):
    return [(z * 4 + (end - step) % 4, z * 4 + end) for z in range(8) for end in (0, 3)]


def z_across():
    pair = (6, 7, 4, 5, 2, 3, 0, 1)
    return [(z * 4 + y, pair[z] * 4 + y) for z in range(8) for y in range(4)]


def z_mirror(bits):
    return [(z * 4 + y, (z ^ bits) * 4 + y) for z in range(8) for y in range(4)]


def dot(a, b):
    return jnp.dot(a, b, preferred_element_type=F32)


def dot_rows(a, b):
    return lax.dot_general(a, b, (((0,), (0,)), ((), ())), preferred_element_type=F32)


def call(kernel, outs, specs, scratch=(), limit=16 << 20, work=None):
    cost = work and pl.CostEstimate(flops=work, bytes_accessed=10**7, transcendentals=0)
    return pl.pallas_call(
        kernel,
        out_shape=outs,
        in_specs=specs,
        out_specs=jax.tree.map(lambda _: VMEM, outs),
        scratch_shapes=list(scratch),
        cost_estimate=cost,
        compiler_params=pltpu.CompilerParams(vmem_limit_bytes=limit),
    )


def struct(shape, kind):
    return jax.ShapeDtypeStruct(shape, kind)


def plan_kernel(place, counts, offsets, grads, info, outgoing):
    total = offsets.shape[0]

    def slide_at(row):
        slide = jnp.int32(-1)
        for s in range(total):
            slide += (offsets[s] <= row).astype(jnp.int32)
        return slide

    def slide_for(at, first, last):
        inner = jnp.where(first + at < last, first + at, first)
        return jnp.where(at == 3, last, inner)

    def plan(plane, carry):
        first = slide_at(plane * PLANE)
        last = slide_at(plane * PLANE + PLANE - 1)
        for at in range(4):
            outgoing[plane * 4 + at] = grads[slide_for(at, first, last)]
        return carry

    lax.fori_loop(0, outgoing.shape[0] // 4, plan, 0)
    tile, core = place[0], place[1]
    y, z = lax.rem(tile, 4), lax.div(tile, 4)
    first, last = slide_at(z * PLANE), slide_at(z * PLANE + PLANE - 1)
    slide = slide_for(y, first, last)
    for start, index in ((OWN, slide), (FIRST, first), (LAST, last)):
        info[start] = offsets[index]
        info[start + 1] = offsets[index] + counts[index]
    for r in range(4):
        quarter = lax.rem(y + 4 - r, 4)
        info[BASE + r] = z * PLANE + quarter * ROWS
        info[PLACE + r] = quarter
    inside = (y == 0) | (y == 3) & (last > first) | (first + y < last) & (y < 3)
    after = offsets[jnp.minimum(last + 1, total - 1)]
    info[QUARTER] = y
    info[GRAD] = jnp.where(inside, info[OWN + 1], info[OWN])
    info[EXTRA] = ((y == 0) | (y == 3)).astype(jnp.int32)
    info[END] = jnp.where(last + 1 < total, after, outgoing.shape[0] * ROWS)
    info[ALONE] = (first == last).astype(jnp.int32)
    info[PLACE + 4] = core
    info[COUNT] = counts[slide]


def keep_rows(info, place, r, skip, rows, lanes):
    row = info[BASE + r] + skip + lax.broadcasted_iota(jnp.int32, (rows, lanes), 0)
    return (row >= info[place]) & (row < info[place + 1])


def store_kept(keep, x, out, start):
    rows = x.shape[0]
    for c in range(6):
        cols = slice(c * 128, (c + 1) * 128)
        out[start : start + rows, cols] = jnp.where(keep, x[:, cols], jnp.zeros((), BF))


def sums_kernel(info, x0, x1, top, bottom, x3, first_out, last_out, both, strips):
    line = lax.broadcasted_iota(jnp.int32, (1, PLANE), 1)
    place = jnp.zeros((1, PLANE), jnp.int32)
    for (r, skip, rows), x in zip(PIECES, (x0, x1, top, bottom, x3)):
        keep = keep_rows(info, FIRST, r, skip, rows, 128)
        keep = keep | keep_rows(info, LAST, r, skip, rows, 128)
        store_kept(keep, x, both, r * ROWS + skip)
        inside = (line >= r * ROWS + skip) & (line < r * ROWS + skip + rows)
        place = jnp.where(inside, line - r * ROWS + info[BASE + r], place)
    row = lax.broadcasted_iota(jnp.int32, (6 * STRIP, D), 0)
    col = lax.broadcasted_iota(jnp.int32, (6 * STRIP, D), 1)
    wanted = (row >> 5) * 128 + (row & (STRIP - 1)) + info[QUARTER] * STRIP
    select = jnp.where(col == wanted, 1.0, 0.0).astype(BF)
    chosen = lax.dot_general(
        select, both[...], (((1,), (1,)), ((), ())), preferred_element_type=F32
    )
    for start, out in ((FIRST, first_out), (LAST, last_out)):
        keep = (place >= info[start]) & (place < info[start + 1])
        kept = jnp.where(keep, chosen, 0.0).astype(BF)
        ones = jnp.broadcast_to(jnp.where(keep, 1.0, 0.0), (16, PLANE)).astype(BF)
        strips[...] = dot(jnp.concatenate([kept, ones], axis=0), both[...])
        for slot, (i, j) in enumerate(PAIRS):
            block = strips[i * STRIP : (i + 1) * STRIP, j * 128 : (j + 1) * 128]
            out[slot * STRIP : (slot + 1) * STRIP, :] = block.astype(BF)
        total = strips[6 * STRIP : 6 * STRIP + 8, :]
        high = total.astype(BF).astype(F32)
        low = total - high
        count = lax.broadcasted_iota(jnp.int32, (16, 128), 0)
        tail = jnp.zeros((16, 128), F32)
        for c in range(6):
            cut = slice(c * 128, (c + 1) * 128)
            tail = jnp.where(count == c, high[0:1, cut], tail)
            tail = jnp.where(count == 6 + c, low[0:1, cut], tail)
        out[TAIL:MESSAGE, :] = tail.astype(BF)


def local_kernel(info, x0, x1, top, bottom, x3, local, local_row, own):
    for (r, skip, rows), x in zip(PIECES, (x0, x1, top, bottom, x3)):
        store_kept(keep_rows(info, OWN, r, skip, rows, 128), x, own, r * ROWS + skip)
    for c in range(CHUNKS):
        here = pl.ds(c * CHUNK, CHUNK)
        local[here, :] = dot_rows(own[:, here], own[...])
    local_row[...] = dot(jnp.ones((8, PLANE), BF), own[...])


def flip_kernel(f0, f1, top, bottom, f3, out):
    start = 0
    for f in (f0, f1, top, bottom, f3):
        rows = f.shape[0]
        for c in range(DIN // CHUNK):
            here = pl.ds(c * CHUNK, CHUNK)
            out[here, start : start + rows] = f[:, here].astype(F32).T.astype(BF)
        start += rows


def fold_kernel(g1, g3, top, bottom, back, ahead):
    half = ROWS // 2
    back[0:half, :] = g1[0:half, :]
    back[half:ROWS, :] = g1[half:ROWS, :] + bottom[...]
    ahead[0:half, :] = g3[0:half, :] + top[...]
    ahead[half:ROWS, :] = g3[half:ROWS, :]


def extras_kernel(info, left_1, right_1, left_2, right_2, *outs):
    start = info[BASE] - info[QUARTER] * ROWS
    keeps = (
        info[FIRST] < start,
        info[END] > start + PLANE,
        info[FIRST] < start - PLANE,
        info[END] > start + 2 * PLANE,
    )
    values = [
        jnp.where(keep, value[...].astype(F32), 0.0)
        for keep, value in zip(keeps, (left_1, right_1, left_2, right_2))
    ]
    before = values[0] + values[2]
    after = values[1] + values[3]
    to_first = jnp.where(info[ALONE] > 0, before + after, before).astype(BF)
    to_last = after.astype(BF)
    for step, out in enumerate(outs):
        last = lax.rem(info[QUARTER] + step, 4) == 3

        @pl.when(last)
        def _():
            out[...] = to_last

        @pl.when(jnp.logical_not(last))
        def _():
            out[...] = to_first


def half_kernel(grads, out):
    for i in range(CHUNKS):
        for j in range(i, CHUNKS):
            rows = pl.ds(i * CHUNK, CHUNK)
            cols = pl.ds(j * CHUNK, CHUNK)
            upper = grads[rows, cols].astype(F32)
            lower = grads[cols, rows].astype(F32)
            block = 0.5 * (upper + lower.T)
            out[rows, cols] = block
            if i != j:
                out[cols, rows] = block.T


def total_of(value):
    return jnp.sum(value, axis=(0, 1), keepdims=True)


def pool_kernel(
    info, local, local_row, e0, e1, e2, e3, half, x0, x1, xt, xb, x3, g0, g1, gt, gb, g3,
    blocks, covar, wide_a, wide_b, mean_col, mean_row, scaled_b, first_b, top_b, second_b, under_b, grad_b,
):
    inverse = 1.0 / jnp.full((1, 1), info[COUNT], jnp.int32).astype(F32)
    covar[...] = local[...]
    mean_row[...] = local_row[...]

    @pl.when(info[EXTRA] > 0)
    def _():
        for r, extra in enumerate((e0, e1, e2, e3)):
            for slot in range(len(PAIRS)):
                row = pl.multiple_of(slot * 128 + info[PLACE + r] * STRIP, STRIP)
                piece = extra[slot * STRIP : (slot + 1) * STRIP, :]
                blocks[pl.ds(row, STRIP), :] = piece.astype(F32)
        for slot, (i, j) in enumerate(PAIRS):
            block = blocks[slot * 128 : (slot + 1) * 128, :]
            rows, cols = pl.ds(i * 128, 128), pl.ds(j * 128, 128)
            covar[rows, cols] += block
            if i != j:
                covar[cols, rows] += block.T

        tail = e0[TAIL:MESSAGE, :].astype(F32)
        for c in range(6):
            cut = pl.ds(c * 128, 128)
            mean_row[:, cut] += tail[c : c + 1, :] + tail[6 + c : 7 + c, :]

    mean_row[...] = mean_row[...] * inverse
    mean_col[...] = mean_row[...].T
    def each(body, start=0):
        def step(c, carry):
            return body(pl.ds(pl.multiple_of(c * CHUNK, CHUNK), CHUNK), carry)

        return lax.fori_loop(0, CHUNKS, step, start)

    def center(here, squares):
        value = covar[here, :] * inverse - mean_col[here, 0:1] * mean_row[0:1, :]
        covar[here, :] = value
        return squares + total_of(value * value)

    squares = each(center, jnp.zeros((1, 1), F32))
    norm = jnp.sqrt(squares + 1e-6)
    over = 1.0 / norm
    root = jnp.sqrt(norm)

    def scale_both(here, carry):
        scaled_b[here, :] = (covar[here, :] * over).astype(BF)
        top_b[here, :] = (half[here, :] * root).astype(BF)
        return carry

    each(scale_both)

    def make_first(here, carry):
        value = (1.5 * over) * covar[here, :] - 0.5 * dot(scaled_b[here, :], scaled_b[...])
        wide_a[here, :] = value
        first_b[here, :] = value.astype(BF)
        return carry

    each(make_first)

    def make_second(here, carry):
        value = 1.5 * wide_a[here, :] - 0.5 * dot(scaled_b[here, :], first_b[...])
        second_b[here, :] = value.astype(BF)
        under_b[here, :] = dot(first_b[here, :], top_b[...]).astype(BF)
        return carry

    each(make_second)

    def make_grad(here, sums):
        top = half[here, :] * root
        right = dot(top_b[here, :], second_b[...])
        sums += 1.5 * total_of(top * wide_a[here, :])
        sums -= 0.5 * total_of(right * first_b[here, :].astype(F32))
        value = 1.5 * top - 0.5 * (right + dot(second_b[here, :], top_b[...]))
        wide_b[here, :] = value
        grad_b[here, :] = value.astype(BF)
        return sums

    sums = each(make_grad, jnp.zeros((1, 1), F32))

    def make_scaled(here, inner):
        value = 1.5 * wide_b[here, :] + 0.25 * dot(under_b[here, :], first_b[...])
        value -= 0.5 * (dot(grad_b[here, :], scaled_b[...]) + dot(scaled_b[here, :], grad_b[...]))
        wide_a[here, :] = value
        return inner + total_of(value * covar[here, :])

    inner = each(make_scaled, jnp.zeros((1, 1), F32))
    grad_norm = sums * (0.5 * over) - inner * over * over
    scale = 2.0 * over * inverse

    def make_sym(here, mean_grad):
        value = (wide_a[here, :] + grad_norm * covar[here, :]) * scale
        second_b[here, :] = value.astype(BF)
        return mean_grad - jnp.sum(value * mean_col[here, 0:1], axis=0, keepdims=True)

    mean_grad = each(make_sym, jnp.zeros((1, D), F32))
    xs, gs = (x0, x1, xt, xb, x3), (g0, g1, gt, gb, g3)
    for (r, skip, rows), x, g in zip(PIECES, xs, gs):
        row = info[BASE + r] + skip + lax.broadcasted_iota(jnp.int32, (rows, D), 0)
        keep = (row >= info[OWN]) & (row < info[GRAD])
        value = dot(x[...], second_b[...]) + mean_grad
        g[...] = jnp.where(keep, value, 0.0).astype(BF)


def term_kernel(info, g0, g1, gt, gb, g3, flipped, sent, mine, plane):
    for (r, skip, rows), g in zip(PIECES, (g0, g1, gt, gb, g3)):
        plane[r * ROWS + skip : r * ROWS + skip + rows, :] = g[...]
    core = info[PLACE + 4]
    half = DIN // 2
    for place, out in ((1 - core, sent), (core, mine)):
        for c in range(half // CHUNK):
            here = pl.ds(pl.multiple_of(place * half + c * CHUNK, CHUNK), CHUNK)
            value = dot(flipped[here, :], plane[...])
            out[c * CHUNK : (c + 1) * CHUNK, :] = value.astype(out.dtype)


def split_kernel(place, mine, *refs):
    others, (own, *sends) = refs[: len(refs) - 4], refs[len(refs) - 4 :]
    rows = own.shape[0]

    def piece(step):
        here = pl.ds(pl.multiple_of(lax.rem(place[0] + step, 4) * rows, rows), rows)
        value = mine[here, :].astype(F32)
        for other in others:
            value = value + other[here, :].astype(F32)
        return value

    own[...] = piece(0)
    for step, out in zip((1, 3, 2), sends):
        out[...] = piece(step).astype(BF)


def add_kernel(mine, a, b, c, out):
    value = mine[...] + a[...].astype(F32) + b[...].astype(F32) + c[...].astype(F32)
    out[...] = value.astype(BF)


def four_kernel(own, a, b, c, out):
    near = own[...].astype(F32) + a[...].astype(F32)
    out[...] = (near + (b[...].astype(F32) + c[...].astype(F32))).astype(BF)


def two_kernel(own, other, out):
    out[...] = (own[...].astype(F32) + other[...].astype(F32)).astype(BF)


def join_kernel(place, own, a, b, c, out):
    rows = own.shape[0]
    for step, value in ((0, own), (1, a), (3, b), (2, c)):
        index = lax.rem(place[0] + 4 - step, 4)
        out[pl.ds(pl.multiple_of(index * rows, rows), rows), :] = value[...]


def final_kernel(core, own, other, out):
    rows = own.shape[0]
    out[pl.ds(pl.multiple_of(core[0] * rows, rows), rows), :] = own[...].astype(F32)
    out[pl.ds(pl.multiple_of((1 - core[0]) * rows, rows), rows), :] = other[...].astype(F32)


def three(values, axis, shift):
    return [lax.ppermute(v, axis, shift(step)) for step, v in zip((1, 3, 2), values)]


def reduce_everywhere(sent, mine, row_grads, core, x_place, y_place):
    g0, g1, top, bottom, g3 = row_grads
    top = lax.ppermute(top, "tile", y_shift(1))
    bottom = lax.ppermute(bottom, "tile", y_shift(-1))
    core, x_place, y_place = core[None], x_place[None], y_place[None]

    def pieces(rows):
        return [struct((rows, D), F32)] + [struct((rows, D), BF)] * 3

    got = lax.ppermute(sent, "grp", CORE_PAIRS)
    own, *sends = call(split_kernel, pieces(128), [SMEM, VMEM, VMEM])(x_place, mine, got)
    got = three(sends, "grp", x_shift)
    got, top, bottom = lax.optimization_barrier((got, top, bottom))
    back, ahead = call(fold_kernel, [struct((ROWS, D), BF)] * 2, [VMEM] * 4)(g1, g3, top, bottom)
    own, *sends = call(split_kernel, pieces(32), [SMEM] + [VMEM] * 4)(y_place, own, *got)
    got = three(sends, "tile", y_shift)
    got, back, ahead = lax.optimization_barrier((got, back, ahead))
    value = call(add_kernel, struct((32, D), BF), [VMEM] * 4)(own, *got)
    home = [lax.ppermute(back, "tile", y_shift(-1)), lax.ppermute(ahead, "tile", y_shift(1))]
    got = [lax.ppermute(value, "tile", z_mirror(bits)) for bits in (1, 2, 3)]
    value = call(four_kernel, struct((32, D), BF), [VMEM] * 4)(value, *got)
    got = lax.ppermute(value, "tile", z_across())
    value = call(two_kernel, struct((32, D), BF), [VMEM] * 2)(value, got)
    value, home = lax.optimization_barrier((value, home))
    got = three([value] * 3, "tile", y_shift)
    value = call(join_kernel, struct((128, D), BF), [SMEM] + [VMEM] * 4)(y_place, value, *got)
    got = three([value] * 3, "grp", x_shift)
    value = call(join_kernel, struct((512, D), BF), [SMEM] + [VMEM] * 4)(x_place, value, *got)
    got = lax.ppermute(value, "grp", CORE_PAIRS)
    return call(final_kernel, struct((DIN, D), F32), [SMEM, VMEM, VMEM])(core, value, got), g0 + home[0] + home[1]


def shards(features, projection, pooled_grad, slide_counts, slide_offsets):
    group = lax.axis_index("grp")
    tile = lax.axis_index("tile")
    core, x_place = group % 2, group // 2
    y = tile % 4
    tiles = lax.axis_size("tile")
    info, outgoing = pl.pallas_call(
        plan_kernel,
        out_shape=[
            struct((SCALARS,), jnp.int32),
            struct((tiles,) + pooled_grad.shape[1:], BF),
        ],
        in_specs=[SMEM] * 3 + [VMEM],
        out_specs=[SMEM, VMEM],
        compiler_params=pltpu.CompilerParams(vmem_limit_bytes=16 << 20),
    )(jnp.stack([tile, core]).astype(jnp.int32), slide_counts, slide_offsets, pooled_grad)
    grads = lax.all_to_all(outgoing, "tile", 0, 0, tiled=True).reshape(D, D)

    half_rows = ROWS // 2

    def around_y(value):
        behind = lax.ppermute(value, "tile", y_shift(1))
        ahead = lax.ppermute(value, "tile", y_shift(-1))
        top = lax.ppermute(behind[:half_rows], "tile", y_shift(1))
        bottom = lax.ppermute(ahead[half_rows:], "tile", y_shift(-1))
        return value, behind, top, bottom, ahead

    pieces = around_y(features)
    mixed = [dot(piece, projection).astype(BF) for piece in pieces]
    message = struct((MESSAGE, 128), BF)
    first_part, last_part = call(
        sums_kernel,
        [message, message],
        [SMEM] + [VMEM] * 5,
        [pltpu.VMEM((PLANE, D), BF), pltpu.VMEM((6 * STRIP + 16, D), F32)],
        work=WORK,
    )(info, *mixed)
    local, local_row = call(
        local_kernel,
        [struct((D, D), F32), struct((8, D), F32)],
        [SMEM] + [VMEM] * 5,
        [pltpu.VMEM((PLANE, D), BF)],
        work=WORK,
    )(info, *mixed)
    flipped = call(flip_kernel, struct((DIN, PLANE), BF), [VMEM] * 5, work=WORK)(
        *pieces
    )

    around = [
        lax.ppermute(last_part, "tile", z_shift(1)),
        lax.ppermute(first_part, "tile", z_shift(-1)),
        lax.ppermute(last_part, "tile", z_shift(2)),
        lax.ppermute(first_part, "tile", z_shift(-2)),
    ]
    half = call(half_kernel, struct((D, D), F32), [VMEM])(grads)
    half, *around = lax.optimization_barrier((half, *around))
    extras = call(extras_kernel, [message] * 4, [SMEM] + [VMEM] * 4, work=WORK)(info, *around)
    extras = list(extras[:1]) + [
        lax.ppermute(extra, "tile", y_to_ends(step)) for step, extra in zip((1, 2, 3), extras[1:])
    ]

    wide = pltpu.VMEM((D, D), F32)
    narrow = pltpu.VMEM((D, D), BF)
    row_grads = call(
        pool_kernel,
        [struct((rows, D), BF) for _, _, rows in PIECES],
        [SMEM] + [VMEM] * 12,
        [pltpu.VMEM((len(PAIRS) * 128, 128), F32)] + [wide] * 3 + [pltpu.VMEM((D, 8), F32), pltpu.VMEM((8, D), F32)] + [narrow] * 6,
        26 << 20,
        WORK,
    )(info, local, local_row, *extras, half, *mixed)
    sent, mine = call(
        term_kernel,
        [struct((512, D), BF), struct((512, D), BF)],
        [SMEM] + [VMEM] * 6,
        [pltpu.VMEM((PLANE, D), BF)],
        work=WORK,
    )(info, *row_grads, flipped)

    projection_grad, row_grad = reduce_everywhere(sent, mine, row_grads, core, x_place, y)
    feature_grad = jnp.einsum(
        "rd,kd->rk", row_grad, projection, preferred_element_type=F32
    ).astype(BF)
    return (feature_grad, projection_grad)


def solution(mesh):
    placed = (P(("grp", "tile"), None), P(), P("grp", "tile", None), P("grp"), P("grp"))
    return jax.shard_map(
        shards,
        mesh=mesh,
        in_specs=placed,
        out_specs=(P(("grp", "tile"), None), P()),
        check_vma=False,
    )
```

profile of v0, /device:TPU:1, one launch (start us, length us, event | category | flops | bytes accessed | tf_op | source)
XLA Modules:
  0.0 164.8 jit_solution(6634955433491146159)
XLA Ops:
  0.6 2.2 %collective-permute-start = (bf16[256,1024]{1,0:T(8,128)(2,1)}, bf16[256,1024]{1,0:T(8,128)(2,1)S(1)}, u32[]{:S(2)}, u32[]{:S(2)}) collective-permute-start(bf16[256,1024]{1,0:T(8,128)(2,1)} %f0.1), channel_id=1, source_target_pairs={{0,1},{1,2},{2,3},{3,0},{4,5},{5,6},{6,7},{7,4},{8,9},{9,10},{10,1... | collective-permute-start | bytes 1572872 | tf_op jit(solution)/shard_map/ppermute | solution.py:462
  6.8 1.6 shard_map.68
  9.5 9.8 %all-to-all-start = ((bf16[32,24,768]{2,1,0:T(8,128)(2,1)}), bf16[32,24,768]{2,1,0:T(8,128)(2,1)S(1)}, u32[]{:S(2)}, u32[]{:S(2)}) async-start(bf16[32,24,768]{2,1,0:T(8,128)(2,1)} %copy-done.1), calls=%async_computation | async-start | bytes 2359296 | tf_op jit(solution)/shard_map/all_to_all | solution.py:457
  19.3 1.6 convolution_convert_fusion.3.x0
  25.6 1.6 convolution_convert_fusion.2.x1
  27.2 1.8 %convolution_convert_fusion.1.x3 = bf16[256,768]{1,0:T(8,128)(2,1)S(1)} fusion(bf16[256,1024]{1,0:T(8,128)(2,1)} %collective-permute-done.2.f3, bf16[1024,768]{1,0:T(8,128)(2,1)S(1)} %copy-done), kind=kOutput, calls=%fused_computation.1 | convolution fusion | flops 402849792 | bytes 2490368 | tf_op jit(solution)/shard_map/dot_general | solution.py:59
  29.0 5.7 %collective-permute-done.1.top = bf16[128,1024]{1,0:T(8,128)(2,1)S(1)} collective-permute-done((bf16[128,1024]{1,0:T(8,128)(2,1)S(1)}, bf16[128,1024]{1,0:T(8,128)(2,1)S(1)}, u32[]{:S(2)}, u32[]{:S(2)}) %collective-permute-start.1) | collective-permute-done | bytes 262176 | tf_op jit(solution)/shard_map/ppermute | solution.py:464
  35.5 2.9 %shard_map.71 = (bf16[688,128]{1,0:T(8,128)(2,1)}, bf16[688,128]{1,0:T(8,128)(2,1)}) custom-call(s32[21]{0:T(128)S(1)} %get-tuple-element.47.info, bf16[256,768]{1,0:T(8,128)(2,1)S(1)} %convolution_convert_fusion.3.x0, bf16[256,768]{1,0:T(8,128)(2,1)S(1)} %convolution_convert_fusion.2.x1, bf16[128,768]{1,0:T(8,128)(2,1)S(1)} %convolution_convert_fusion.5.top.xt, ...), custom_call_target="tpu_custom_call" | custom-call | flops 5000000000 | bytes 10000000 | tf_op jit(solution)/shard_map/pallas_call | solution.py:471
  38.4 1.8 %collective-permute-start.4 = (bf16[688,128]{1,0:T(8,128)(2,1)}, bf16[688,128]{1,0:T(8,128)(2,1)S(1)}, u32[]{:S(2)}, u32[]{:S(2)}) collective-permute-start(bf16[688,128]{1,0:T(8,128)(2,1)} %get-tuple-element.51), channel_id=1, source_target_pairs={{0,4},{1,5},{2,6},{3,7},{4,8},{5,9},{6,10},{7,11},{8,12},{9,13},{1... | collective-permute-start | bytes 528392 | tf_op jit(solution)/shard_map/ppermute | solution.py:490
  41.6 2.6 %collective-permute-start.5 = (bf16[688,128]{1,0:T(8,128)(2,1)}, bf16[688,128]{1,0:T(8,128)(2,1)}, u32[]{:S(2)}, u32[]{:S(2)}) collective-permute-start(bf16[688,128]{1,0:T(8,128)(2,1)} %get-tuple-element.52), channel_id=1, source_target_pairs={{0,28},{1,29},{2,30},{3,31},{4,0},{5,1},{6,2},{7,3},{8,4},{9,5},{1... | collective-permute-start | bytes 528392 | tf_op jit(solution)/shard_map/ppermute | solution.py:491
  45.1 2.4 %shard_map.69 = (f32[768,768]{1,0:T(8,128)S(1)}, f32[8,768]{1,0:T(8,128)S(1)}) custom-call(s32[21]{0:T(128)S(1)} %get-tuple-element.47.info, bf16[256,768]{1,0:T(8,128)(2,1)S(1)} %convolution_convert_fusion.3.x0, bf16[256,768]{1,0:T(8,128)(2,1)S(1)} %convolution_convert_fusion.2.x1, bf16[128,768]{1,0:T(8,128)(2,1)S(1)} %convolution_convert_fusion.5.top.xt, ...), custom_call_target="tpu_custom_call" | custom-call | flops 5000000000 | bytes 10000000 | tf_op jit(solution)/shard_map/pallas_call | solution.py:478
  50.7 6.3 %collective-permute-done.6.left_2 = bf16[688,128]{1,0:T(8,128)(2,1)} collective-permute-done((bf16[688,128]{1,0:T(8,128)(2,1)}, bf16[688,128]{1,0:T(8,128)(2,1)}, u32[]{:S(2)}, u32[]{:S(2)}) %collective-permute-start.6) | collective-permute-done | bytes 176160 | tf_op jit(solution)/shard_map/ppermute | solution.py:492
  61.1 5.5 %collective-permute-start.10 = (bf16[688,128]{1,0:T(8,128)(2,1)S(1)}, bf16[688,128]{1,0:T(8,128)(2,1)S(1)}, u32[]{:S(2)}, u32[]{:S(2)}) collective-permute-start(bf16[688,128]{1,0:T(8,128)(2,1)S(1)} %get-tuple-element.60), channel_id=1, source_target_pairs={{1,0},{0,3},{5,4},{4,7},{9,8},{8,11},{13,12},{12,15},{17,16},{16,1... | collective-permute-start | bytes 528392 | tf_op jit(solution)/shard_map/ppermute | solution.py:499
  66.6 1.7 %shard_map.74.flipped = bf16[1024,1024]{1,0:T(8,128)(2,1)S(1)} custom-call(bf16[256,1024]{1,0:T(8,128)(2,1)S(1)} %copy-done.17, bf16[256,1024]{1,0:T(8,128)(2,1)S(1)} %copy-done.14, bf16[128,1024]{1,0:T(8,128)(2,1)S(1)} %collective-permute-done.1.top, bf16[128,1024]{1,0:T(8,128)(2,1)S(1)} %collective-permute-done.3.bottom, ...), custom_call_target="tpu_custom_call" | custom-call | flops 5000000000 | bytes 10000000 | tf_op jit(solution)/shard_map/pallas_call | solution.py:485
  70.6 15.5 %shard_map.73 = (bf16[256,768]{1,0:T(8,128)(2,1)S(1)}, bf16[256,768]{1,0:T(8,128)(2,1)S(1)}, bf16[128,768]{1,0:T(8,128)(2,1)S(1)}, bf16[128,768]{1,0:T(8,128)(2,1)S(1)}, bf16[256,768]{1,0:T(8,128)(2,1)S(1)}) custom-call(s32[21]{0:T(128)S(1)} %get-tuple-element.47.info, f32[768,768]{1,0:T(8,128)S(1)} %copy-done.27, f32[8,768]{1,0:T(8,128)S(1)} %get-tuple-element.49.local_row, ...), custom_call_target="tpu_custom_call" | custom-call | flops 5000000000 | bytes 10000000 | tf_op jit(solution)/shard_map/pallas_call | solution.py:504
  86.1 3.0 %shard_map.75 = (bf16[512,768]{1,0:T(8,128)(2,1)}, bf16[512,768]{1,0:T(8,128)(2,1)S(1)}) custom-call(s32[21]{0:T(128)S(1)} %get-tuple-element.47.info, bf16[256,768]{1,0:T(8,128)(2,1)S(1)} %get-tuple-element.62.g0, bf16[256,768]{1,0:T(8,128)(2,1)S(1)} %get-tuple-element.63.g1, bf16[128,768]{1,0:T(8,128)(2,1)S(1)} %get-tuple-element.64.gt, ...), custom_call_target="tpu_custom_call" | custom-call | flops 5000000000 | bytes 10000000 | tf_op jit(solution)/shard_map/pallas_call | solution.py:512
  89.2 4.7 %collective-permute-start.11 = (bf16[512,768]{1,0:T(8,128)(2,1)}, bf16[512,768]{1,0:T(8,128)(2,1)S(1)}, u32[]{:S(2)}, u32[]{:S(2)}) collective-permute-start(bf16[512,768]{1,0:T(8,128)(2,1)} %get-tuple-element.68), channel_id=1, source_target_pairs={{0,32},{32,0},{64,96},{96,64},{128,160},{160,128},{192,224},{224,1... | collective-permute-start | bytes 2359304 | tf_op jit(solution)/shard_map/ppermute | solution.py:418
  93.9 2.7 %collective-permute-start.16 = (bf16[128,768]{1,0:T(8,128)(2,1)}, bf16[128,768]{1,0:T(8,128)(2,1)}, u32[]{:S(2)}, u32[]{:S(2)}) collective-permute-start(bf16[128,768]{1,0:T(8,128)(2,1)} %copy-done.18), channel_id=1, source_target_pairs={{0,3},{1,0},{2,1},{3,2},{4,7},{5,4},{6,5},{7,6},{8,11},{9,8},{10,9... | collective-permute-start | bytes 589832 | tf_op jit(solution)/shard_map/ppermute | solution.py:412
  102.4 3.0 %collective-permute-done.12.refs_0_ = bf16[128,768]{1,0:T(8,128)(2,1)S(1)} collective-permute-done((bf16[128,768]{1,0:T(8,128)(2,1)}, bf16[128,768]{1,0:T(8,128)(2,1)S(1)}, u32[]{:S(2)}, u32[]{:S(2)}) %collective-permute-start.12) | collective-permute-done | bytes 196640 | tf_op jit(solution)/shard_map/ppermute | solution.py:406
  105.4 5.2 %collective-permute-done.14.refs_2_ = bf16[128,768]{1,0:T(8,128)(2,1)S(1)} collective-permute-done((bf16[128,768]{1,0:T(8,128)(2,1)}, bf16[128,768]{1,0:T(8,128)(2,1)S(1)}, u32[]{:S(2)}, u32[]{:S(2)}) %collective-permute-start.14) | collective-permute-done | bytes 196640 | tf_op jit(solution)/shard_map/ppermute | solution.py:406
  111.8 2.7 %collective-permute-start.18 = (bf16[32,768]{1,0:T(8,128)(2,1)S(1)}, bf16[32,768]{1,0:T(8,128)(2,1)S(1)}, u32[]{:S(2)}, u32[]{:S(2)}) collective-permute-start(bf16[32,768]{1,0:T(8,128)(2,1)S(1)} %get-tuple-element.78), channel_id=1, source_target_pairs={{0,3},{1,0},{2,1},{3,2},{4,7},{5,4},{6,5},{7,6},{8,11},{9,8},{10,9... | collective-permute-start | bytes 147464 | tf_op jit(solution)/shard_map/ppermute | solution.py:406
  120.4 2.6 %collective-permute-start.20 = (bf16[32,768]{1,0:T(8,128)(2,1)S(1)}, bf16[32,768]{1,0:T(8,128)(2,1)S(1)}, u32[]{:S(2)}, u32[]{:S(2)}) collective-permute-start(bf16[32,768]{1,0:T(8,128)(2,1)S(1)} %shard_map.79.own), channel_id=1, source_target_pairs={{0,4},{1,5},{2,6},{3,7},{4,0},{5,1},{6,2},{7,3},{8,12},{9,13},{10,... | collective-permute-start | bytes 147464 | tf_op jit(solution)/shard_map/ppermute | solution.py:428
  123.0 2.1 %collective-permute-start.21 = (bf16[32,768]{1,0:T(8,128)(2,1)S(1)}, bf16[32,768]{1,0:T(8,128)(2,1)S(1)}, u32[]{:S(2)}, u32[]{:S(2)}) collective-permute-start(bf16[32,768]{1,0:T(8,128)(2,1)S(1)} %shard_map.79.own), channel_id=1, source_target_pairs={{0,8},{1,9},{2,10},{3,11},{4,12},{5,13},{6,14},{7,15},{8,0},{9,1},... | collective-permute-start | bytes 147464 | tf_op jit(solution)/shard_map/ppermute | solution.py:428
  126.8 3.0 %collective-permute-done.22.c = bf16[32,768]{1,0:T(8,128)(2,1)S(1)} collective-permute-done((bf16[32,768]{1,0:T(8,128)(2,1)S(1)}, bf16[32,768]{1,0:T(8,128)(2,1)S(1)}, u32[]{:S(2)}, u32[]{:S(2)}) %collective-permute-start.22) | collective-permute-done | bytes 49184 | tf_op jit(solution)/shard_map/ppermute | solution.py:428
  130.6 4.7 %collective-permute-done.23.other = bf16[32,768]{1,0:T(8,128)(2,1)S(1)} collective-permute-done((bf16[32,768]{1,0:T(8,128)(2,1)S(1)}, bf16[32,768]{1,0:T(8,128)(2,1)S(1)}, u32[]{:S(2)}, u32[]{:S(2)}) %collective-permute-start.23) | collective-permute-done | bytes 49184 | tf_op jit(solution)/shard_map/ppermute | solution.py:430
  135.7 2.3 %collective-permute-start.27 = (bf16[32,768]{1,0:T(8,128)(2,1)S(1)}, bf16[32,768]{1,0:T(8,128)(2,1)S(1)}, u32[]{:S(2)}, u32[]{:S(2)}) collective-permute-start(bf16[32,768]{1,0:T(8,128)(2,1)S(1)} %shard_map.81.own), channel_id=1, source_target_pairs={{0,3},{1,0},{2,1},{3,2},{4,7},{5,4},{6,5},{7,6},{8,11},{9,8},{10,9... | collective-permute-start | bytes 147464 | tf_op jit(solution)/shard_map/ppermute | solution.py:406
  139.5 3.0 %collective-permute-done.28.c = bf16[32,768]{1,0:T(8,128)(2,1)S(1)} collective-permute-done((bf16[32,768]{1,0:T(8,128)(2,1)S(1)}, bf16[32,768]{1,0:T(8,128)(2,1)S(1)}, u32[]{:S(2)}, u32[]{:S(2)}) %collective-permute-start.28) | collective-permute-done | bytes 49184 | tf_op jit(solution)/shard_map/ppermute | solution.py:406
  143.1 2.2 %collective-permute-start.30 = (bf16[128,768]{1,0:T(8,128)(2,1)S(1)}, bf16[128,768]{1,0:T(8,128)(2,1)S(1)}, u32[]{:S(2)}, u32[]{:S(2)}) collective-permute-start(bf16[128,768]{1,0:T(8,128)(2,1)S(1)} %shard_map.82.own), channel_id=1, source_target_pairs={{0,192},{32,224},{64,0},{96,32},{128,64},{160,96},{192,128},{224,1... | collective-permute-start | bytes 589832 | tf_op jit(solution)/shard_map/ppermute | solution.py:406
  145.3 3.1 %collective-permute-done.29.a = bf16[128,768]{1,0:T(8,128)(2,1)S(1)} collective-permute-done((bf16[128,768]{1,0:T(8,128)(2,1)S(1)}, bf16[128,768]{1,0:T(8,128)(2,1)S(1)}, u32[]{:S(2)}, u32[]{:S(2)}) %collective-permute-start.29) | collective-permute-done | bytes 196640 | tf_op jit(solution)/shard_map/ppermute | solution.py:406
  148.3 1.7 %collective-permute-done.30.b = bf16[128,768]{1,0:T(8,128)(2,1)S(1)} collective-permute-done((bf16[128,768]{1,0:T(8,128)(2,1)S(1)}, bf16[128,768]{1,0:T(8,128)(2,1)S(1)}, u32[]{:S(2)}, u32[]{:S(2)}) %collective-permute-start.30) | collective-permute-done | bytes 196640 | tf_op jit(solution)/shard_map/ppermute | solution.py:406
  151.4 9.6 %collective-permute-start.32 = (bf16[512,768]{1,0:T(8,128)(2,1)S(1)}, bf16[512,768]{1,0:T(8,128)(2,1)S(1)}, u32[]{:S(2)}, u32[]{:S(2)}) collective-permute-start(bf16[512,768]{1,0:T(8,128)(2,1)S(1)} %shard_map.83.own), channel_id=1, source_target_pairs={{0,32},{32,0},{64,96},{96,64},{128,160},{160,128},{192,224},{224,1... | collective-permute-start | bytes 2359304 | tf_op jit(solution)/shard_map/ppermute | solution.py:437
  162.9 1.9 %shard_map.84 = f32[1024,768]{1,0:T(8,128)} custom-call(s32[1]{0:T(128)} %bitcast.1.core, bf16[512,768]{1,0:T(8,128)(2,1)S(1)} %shard_map.83.own, bf16[512,768]{1,0:T(8,128)(2,1)S(1)} %collective-permute-done.32.other), custom_call_target="tpu_custom_call" | custom-call | tf_op jit(solution)/shard_map/pallas_call | solution.py:438
  (118 shorter events, 43.4 us)
Async XLA Ops:
  0.6 20.3 %collective-permute-start = (bf16[256,1024]{1,0:T(8,128)(2,1)}, bf16[256,1024]{1,0:T(8,128)(2,1)S(1)}, u32[]{:S(2)}, u32[]{:S(2)}) collective-permute-start(bf16[256,1024]{1,0:T(8,128)(2,1)} %f0.1), channel_id=1, source_target_pairs={{0,1},{1,2},{2,3},{3,0},{4,5},{5,6},{6,7},{7,4},{8,9},{9,10},{10,1... | collective-permute-start | bytes 1572872 | tf_op jit(solution)/shard_map/ppermute | solution.py:462
  2.8 20.2 %collective-permute-start.2 = (bf16[256,1024]{1,0:T(8,128)(2,1)}, bf16[256,1024]{1,0:T(8,128)(2,1)}, u32[]{:S(2)}, u32[]{:S(2)}) collective-permute-start(bf16[256,1024]{1,0:T(8,128)(2,1)} %f0.1), channel_id=1, source_target_pairs={{0,3},{1,0},{2,1},{3,2},{4,7},{5,4},{6,5},{7,6},{8,11},{9,8},{10,9... | collective-permute-start | bytes 1572872 | tf_op jit(solution)/shard_map/ppermute | solution.py:463
  9.5 40.2 %all-to-all-start = ((bf16[32,24,768]{2,1,0:T(8,128)(2,1)}), bf16[32,24,768]{2,1,0:T(8,128)(2,1)S(1)}, u32[]{:S(2)}, u32[]{:S(2)}) async-start(bf16[32,24,768]{2,1,0:T(8,128)(2,1)} %copy-done.1), calls=%async_computation | async-start | bytes 2359296 | tf_op jit(solution)/shard_map/all_to_all | solution.py:457
  21.8 12.9 %collective-permute-start.1 = (bf16[128,1024]{1,0:T(8,128)(2,1)S(1)}, bf16[128,1024]{1,0:T(8,128)(2,1)S(1)}, u32[]{:S(2)}, u32[]{:S(2)}) collective-permute-start(bf16[128,1024]{1,0:T(8,128)(2,1)S(1)} %slice.8), channel_id=1, source_target_pairs={{0,1},{1,2},{2,3},{3,0},{4,5},{5,6},{6,7},{7,4},{8,9},{9,10},{10,1... | collective-permute-start | bytes 786440 | tf_op jit(solution)/shard_map/ppermute | solution.py:464
  24.1 11.0 %collective-permute-start.3 = (bf16[128,1024]{1,0:T(8,128)(2,1)S(1)}, bf16[128,1024]{1,0:T(8,128)(2,1)S(1)}, u32[]{:S(2)}, u32[]{:S(2)}) collective-permute-start(bf16[128,1024]{1,0:T(8,128)(2,1)S(1)} %slice.9), channel_id=1, source_target_pairs={{0,3},{1,0},{2,1},{3,2},{4,7},{5,4},{6,5},{7,6},{8,11},{9,8},{10,9... | collective-permute-start | bytes 786440 | tf_op jit(solution)/shard_map/ppermute | solution.py:465
  38.4 12.3 %collective-permute-start.4 = (bf16[688,128]{1,0:T(8,128)(2,1)}, bf16[688,128]{1,0:T(8,128)(2,1)S(1)}, u32[]{:S(2)}, u32[]{:S(2)}) collective-permute-start(bf16[688,128]{1,0:T(8,128)(2,1)} %get-tuple-element.51), channel_id=1, source_target_pairs={{0,4},{1,5},{2,6},{3,7},{4,8},{5,9},{6,10},{7,11},{8,12},{9,13},{1... | collective-permute-start | bytes 528392 | tf_op jit(solution)/shard_map/ppermute | solution.py:490
  40.1 16.9 %collective-permute-start.6 = (bf16[688,128]{1,0:T(8,128)(2,1)}, bf16[688,128]{1,0:T(8,128)(2,1)}, u32[]{:S(2)}, u32[]{:S(2)}) collective-permute-start(bf16[688,128]{1,0:T(8,128)(2,1)} %get-tuple-element.51), channel_id=1, source_target_pairs={{0,8},{1,9},{2,10},{3,11},{4,12},{5,13},{6,14},{7,15},{8,16},{9,17... | collective-permute-start | bytes 528392 | tf_op jit(solution)/shard_map/ppermute | solution.py:492
  41.6 9.1 %collective-permute-start.5 = (bf16[688,128]{1,0:T(8,128)(2,1)}, bf16[688,128]{1,0:T(8,128)(2,1)}, u32[]{:S(2)}, u32[]{:S(2)}) collective-permute-start(bf16[688,128]{1,0:T(8,128)(2,1)} %get-tuple-element.52), channel_id=1, source_target_pairs={{0,28},{1,29},{2,30},{3,31},{4,0},{5,1},{6,2},{7,3},{8,4},{9,5},{1... | collective-permute-start | bytes 528392 | tf_op jit(solution)/shard_map/ppermute | solution.py:491
  44.2 12.8 %collective-permute-start.7 = (bf16[688,128]{1,0:T(8,128)(2,1)}, bf16[688,128]{1,0:T(8,128)(2,1)}, u32[]{:S(2)}, u32[]{:S(2)}) collective-permute-start(bf16[688,128]{1,0:T(8,128)(2,1)} %get-tuple-element.52), channel_id=1, source_target_pairs={{0,24},{1,25},{2,26},{3,27},{4,28},{5,29},{6,30},{7,31},{8,0},{9,1... | collective-permute-start | bytes 528392 | tf_op jit(solution)/shard_map/ppermute | solution.py:493
  58.4 9.9 %collective-permute-start.8 = (bf16[688,128]{1,0:T(8,128)(2,1)S(1)}, bf16[688,128]{1,0:T(8,128)(2,1)S(1)}, u32[]{:S(2)}, u32[]{:S(2)}) collective-permute-start(bf16[688,128]{1,0:T(8,128)(2,1)S(1)} %get-tuple-element.58), channel_id=1, source_target_pairs={{3,0},{2,3},{7,4},{6,7},{11,8},{10,11},{15,12},{14,15},{19,16},{18... | collective-permute-start | bytes 528392 | tf_op jit(solution)/shard_map/ppermute | solution.py:499
  59.7 9.7 %collective-permute-start.9 = (bf16[688,128]{1,0:T(8,128)(2,1)S(1)}, bf16[688,128]{1,0:T(8,128)(2,1)S(1)}, u32[]{:S(2)}, u32[]{:S(2)}) collective-permute-start(bf16[688,128]{1,0:T(8,128)(2,1)S(1)} %get-tuple-element.59), channel_id=1, source_target_pairs={{2,0},{1,3},{6,4},{5,7},{10,8},{9,11},{14,12},{13,15},{18,16},{17,... | collective-permute-start | bytes 528392 | tf_op jit(solution)/shard_map/ppermute | solution.py:499
  61.1 9.4 %collective-permute-start.10 = (bf16[688,128]{1,0:T(8,128)(2,1)S(1)}, bf16[688,128]{1,0:T(8,128)(2,1)S(1)}, u32[]{:S(2)}, u32[]{:S(2)}) collective-permute-start(bf16[688,128]{1,0:T(8,128)(2,1)S(1)} %get-tuple-element.60), channel_id=1, source_target_pairs={{1,0},{0,3},{5,4},{4,7},{9,8},{8,11},{13,12},{12,15},{17,16},{16,1... | collective-permute-start | bytes 528392 | tf_op jit(solution)/shard_map/ppermute | solution.py:499
  89.2 7.4 %collective-permute-start.11 = (bf16[512,768]{1,0:T(8,128)(2,1)}, bf16[512,768]{1,0:T(8,128)(2,1)S(1)}, u32[]{:S(2)}, u32[]{:S(2)}) collective-permute-start(bf16[512,768]{1,0:T(8,128)(2,1)} %get-tuple-element.68), channel_id=1, source_target_pairs={{0,32},{32,0},{64,96},{96,64},{128,160},{160,128},{192,224},{224,1... | collective-permute-start | bytes 2359304 | tf_op jit(solution)/shard_map/ppermute | solution.py:418
  93.9 8.5 %collective-permute-start.15 = (bf16[128,768]{1,0:T(8,128)(2,1)}, bf16[128,768]{1,0:T(8,128)(2,1)}, u32[]{:S(2)}, u32[]{:S(2)}) collective-permute-start(bf16[128,768]{1,0:T(8,128)(2,1)} %copy-done.19), channel_id=1, source_target_pairs={{0,1},{1,2},{2,3},{3,0},{4,5},{5,6},{6,7},{7,4},{8,9},{9,10},{10,1... | collective-permute-start | bytes 589832 | tf_op jit(solution)/shard_map/ppermute | solution.py:411
  93.9 8.5 %collective-permute-start.16 = (bf16[128,768]{1,0:T(8,128)(2,1)}, bf16[128,768]{1,0:T(8,128)(2,1)}, u32[]{:S(2)}, u32[]{:S(2)}) collective-permute-start(bf16[128,768]{1,0:T(8,128)(2,1)} %copy-done.18), channel_id=1, source_target_pairs={{0,3},{1,0},{2,1},{3,2},{4,7},{5,4},{6,5},{7,6},{8,11},{9,8},{10,9... | collective-permute-start | bytes 589832 | tf_op jit(solution)/shard_map/ppermute | solution.py:412
  98.2 7.2 %collective-permute-start.12 = (bf16[128,768]{1,0:T(8,128)(2,1)}, bf16[128,768]{1,0:T(8,128)(2,1)S(1)}, u32[]{:S(2)}, u32[]{:S(2)}) collective-permute-start(bf16[128,768]{1,0:T(8,128)(2,1)} %get-tuple-element.70), channel_id=1, source_target_pairs={{0,64},{32,96},{64,128},{96,160},{128,192},{160,224},{192,0},{224,... | collective-permute-start | bytes 589832 | tf_op jit(solution)/shard_map/ppermute | solution.py:406
  99.4 6.0 %collective-permute-start.13 = (bf16[128,768]{1,0:T(8,128)(2,1)}, bf16[128,768]{1,0:T(8,128)(2,1)S(1)}, u32[]{:S(2)}, u32[]{:S(2)}) collective-permute-start(bf16[128,768]{1,0:T(8,128)(2,1)} %get-tuple-element.71), channel_id=1, source_target_pairs={{0,192},{32,224},{64,0},{96,32},{128,64},{160,96},{192,128},{224,1... | collective-permute-start | bytes 589832 | tf_op jit(solution)/shard_map/ppermute | solution.py:406
  100.9 9.8 %collective-permute-start.14 = (bf16[128,768]{1,0:T(8,128)(2,1)}, bf16[128,768]{1,0:T(8,128)(2,1)S(1)}, u32[]{:S(2)}, u32[]{:S(2)}) collective-permute-start(bf16[128,768]{1,0:T(8,128)(2,1)} %get-tuple-element.72), channel_id=1, source_target_pairs={{0,128},{32,160},{64,192},{96,224},{128,0},{160,32},{192,64},{224,... | collective-permute-start | bytes 589832 | tf_op jit(solution)/shard_map/ppermute | solution.py:406
  111.7 6.5 %collective-permute-start.17 = (bf16[32,768]{1,0:T(8,128)(2,1)S(1)}, bf16[32,768]{1,0:T(8,128)(2,1)S(1)}, u32[]{:S(2)}, u32[]{:S(2)}) collective-permute-start(bf16[32,768]{1,0:T(8,128)(2,1)S(1)} %get-tuple-element.77), channel_id=1, source_target_pairs={{0,1},{1,2},{2,3},{3,0},{4,5},{5,6},{6,7},{7,4},{8,9},{9,10},{10,1... | collective-permute-start | bytes 147464 | tf_op jit(solution)/shard_map/ppermute | solution.py:406
  111.8 6.4 %collective-permute-start.18 = (bf16[32,768]{1,0:T(8,128)(2,1)S(1)}, bf16[32,768]{1,0:T(8,128)(2,1)S(1)}, u32[]{:S(2)}, u32[]{:S(2)}) collective-permute-start(bf16[32,768]{1,0:T(8,128)(2,1)S(1)} %get-tuple-element.78), channel_id=1, source_target_pairs={{0,3},{1,0},{2,1},{3,2},{4,7},{5,4},{6,5},{7,6},{8,11},{9,8},{10,9... | collective-permute-start | bytes 147464 | tf_op jit(solution)/shard_map/ppermute | solution.py:406
  114.5 4.4 %collective-permute-start.19 = (bf16[32,768]{1,0:T(8,128)(2,1)S(1)}, bf16[32,768]{1,0:T(8,128)(2,1)S(1)}, u32[]{:S(2)}, u32[]{:S(2)}) collective-permute-start(bf16[32,768]{1,0:T(8,128)(2,1)S(1)} %get-tuple-element.79), channel_id=1, source_target_pairs={{0,2},{1,3},{2,0},{3,1},{4,6},{5,7},{6,4},{7,5},{8,10},{9,11},{10,... | collective-permute-start | bytes 147464 | tf_op jit(solution)/shard_map/ppermute | solution.py:406
  118.9 16.4 %collective-permute-start.24 = (bf16[256,768]{1,0:T(8,128)(2,1)S(1)}, bf16[256,768]{1,0:T(8,128)(2,1)S(1)}, u32[]{:S(2)}, u32[]{:S(2)}) collective-permute-start(bf16[256,768]{1,0:T(8,128)(2,1)S(1)} %get-tuple-element.87), channel_id=1, source_target_pairs={{0,3},{1,0},{2,1},{3,2},{4,7},{5,4},{6,5},{7,6},{8,11},{9,8},{10,9... | collective-permute-start | bytes 1179656 | tf_op jit(solution)/shard_map/ppermute | solution.py:427
  119.8 15.5 %collective-permute-start.25 = (bf16[256,768]{1,0:T(8,128)(2,1)S(1)}, bf16[256,768]{1,0:T(8,128)(2,1)S(1)}, u32[]{:S(2)}, u32[]{:S(2)}) collective-permute-start(bf16[256,768]{1,0:T(8,128)(2,1)S(1)} %get-tuple-element.88), channel_id=1, source_target_pairs={{0,1},{1,2},{2,3},{3,0},{4,5},{5,6},{6,7},{7,4},{8,9},{9,10},{10,1... | collective-permute-start | bytes 1179656 | tf_op jit(solution)/shard_map/ppermute | solution.py:427
  120.4 5.7 %collective-permute-start.20 = (bf16[32,768]{1,0:T(8,128)(2,1)S(1)}, bf16[32,768]{1,0:T(8,128)(2,1)S(1)}, u32[]{:S(2)}, u32[]{:S(2)}) collective-permute-start(bf16[32,768]{1,0:T(8,128)(2,1)S(1)} %shard_map.79.own), channel_id=1, source_target_pairs={{0,4},{1,5},{2,6},{3,7},{4,0},{5,1},{6,2},{7,3},{8,12},{9,13},{10,... | collective-permute-start | bytes 147464 | tf_op jit(solution)/shard_map/ppermute | solution.py:428
  125.1 4.7 %collective-permute-start.22 = (bf16[32,768]{1,0:T(8,128)(2,1)S(1)}, bf16[32,768]{1,0:T(8,128)(2,1)S(1)}, u32[]{:S(2)}, u32[]{:S(2)}) collective-permute-start(bf16[32,768]{1,0:T(8,128)(2,1)S(1)} %shard_map.79.own), channel_id=1, source_target_pairs={{0,12},{1,13},{2,14},{3,15},{4,8},{5,9},{6,10},{7,11},{8,4},{9,5},... | collective-permute-start | bytes 147464 | tf_op jit(solution)/shard_map/ppermute | solution.py:428
  129.8 5.5 %collective-permute-start.23 = (bf16[32,768]{1,0:T(8,128)(2,1)S(1)}, bf16[32,768]{1,0:T(8,128)(2,1)S(1)}, u32[]{:S(2)}, u32[]{:S(2)}) collective-permute-start(bf16[32,768]{1,0:T(8,128)(2,1)S(1)} %shard_map.80.own), channel_id=1, source_target_pairs={{0,24},{1,25},{2,26},{3,27},{4,28},{5,29},{6,30},{7,31},{8,16},{9,... | collective-permute-start | bytes 147464 | tf_op jit(solution)/shard_map/ppermute | solution.py:430
  135.3 4.2 %collective-permute-start.26 = (bf16[32,768]{1,0:T(8,128)(2,1)S(1)}, bf16[32,768]{1,0:T(8,128)(2,1)S(1)}, u32[]{:S(2)}, u32[]{:S(2)}) collective-permute-start(bf16[32,768]{1,0:T(8,128)(2,1)S(1)} %shard_map.81.own), channel_id=1, source_target_pairs={{0,1},{1,2},{2,3},{3,0},{4,5},{5,6},{6,7},{7,4},{8,9},{9,10},{10,1... | collective-permute-start | bytes 147464 | tf_op jit(solution)/shard_map/ppermute | solution.py:406
  138.1 4.4 %collective-permute-start.28 = (bf16[32,768]{1,0:T(8,128)(2,1)S(1)}, bf16[32,768]{1,0:T(8,128)(2,1)S(1)}, u32[]{:S(2)}, u32[]{:S(2)}) collective-permute-start(bf16[32,768]{1,0:T(8,128)(2,1)S(1)} %shard_map.81.own), channel_id=1, source_target_pairs={{0,2},{1,3},{2,0},{3,1},{4,6},{5,7},{6,4},{7,5},{8,10},{9,11},{10,... | collective-permute-start | bytes 147464 | tf_op jit(solution)/shard_map/ppermute | solution.py:406
  142.5 5.8 %collective-permute-start.29 = (bf16[128,768]{1,0:T(8,128)(2,1)S(1)}, bf16[128,768]{1,0:T(8,128)(2,1)S(1)}, u32[]{:S(2)}, u32[]{:S(2)}) collective-permute-start(bf16[128,768]{1,0:T(8,128)(2,1)S(1)} %shard_map.82.own), channel_id=1, source_target_pairs={{0,64},{32,96},{64,128},{96,160},{128,192},{160,224},{192,0},{224,... | collective-permute-start | bytes 589832 | tf_op jit(solution)/shard_map/ppermute | solution.py:406
  143.1 6.9 %collective-permute-start.30 = (bf16[128,768]{1,0:T(8,128)(2,1)S(1)}, bf16[128,768]{1,0:T(8,128)(2,1)S(1)}, u32[]{:S(2)}, u32[]{:S(2)}) collective-permute-start(bf16[128,768]{1,0:T(8,128)(2,1)S(1)} %shard_map.82.own), channel_id=1, source_target_pairs={{0,192},{32,224},{64,0},{96,32},{128,64},{160,96},{192,128},{224,1... | collective-permute-start | bytes 589832 | tf_op jit(solution)/shard_map/ppermute | solution.py:406
  145.3 6.0 %collective-permute-start.31 = (bf16[128,768]{1,0:T(8,128)(2,1)S(1)}, bf16[128,768]{1,0:T(8,128)(2,1)S(1)}, u32[]{:S(2)}, u32[]{:S(2)}) collective-permute-start(bf16[128,768]{1,0:T(8,128)(2,1)S(1)} %shard_map.82.own), channel_id=1, source_target_pairs={{0,128},{32,160},{64,192},{96,224},{128,0},{160,32},{192,64},{224,... | collective-permute-start | bytes 589832 | tf_op jit(solution)/shard_map/ppermute | solution.py:406
  151.4 11.6 %collective-permute-start.32 = (bf16[512,768]{1,0:T(8,128)(2,1)S(1)}, bf16[512,768]{1,0:T(8,128)(2,1)S(1)}, u32[]{:S(2)}, u32[]{:S(2)}) collective-permute-start(bf16[512,768]{1,0:T(8,128)(2,1)S(1)} %shard_map.83.own), channel_id=1, source_target_pairs={{0,32},{32,0},{64,96},{96,64},{128,160},{160,128},{192,224},{224,1... | collective-permute-start | bytes 2359304 | tf_op jit(solution)/shard_map/ppermute | solution.py:437
  (30 other events, 192.1 us)
where the time goes:
time: 165 us
  starting transfers between devices  70.2 us (43%)
  waiting for transfers between devices  42.1 us (26%)
  Pallas kernels  33.1 us (20%)
  local copies, waits for them, and re-layouts  11.1 us (7%)
  matrix products  7.16 us (4%)
    ppermute x12, waiting for transfers between devices, three(): lax.ppermute(v, axis, shift(step))  18.5 us
    pallas_call x1, Pallas kernels, shards(): call(pool_kernel, [struct((rows, D), BF) for _, _, rows in PIECES], [SMEM...  15.5 us
    ppermute x12, starting transfers between devices, three(): lax.ppermute(v, axis, shift(step))  13.9 us
    unnamed x56, local copies, waits for them, and re-layouts  10.1 us
    all_to_all x1, starting transfers between devices, shards(): grads = lax.all_to_all(outgoing, 'tile', 0, 0, tiled=True).reshape(D, D)  9.84 us
    ppermute x1, starting transfers between devices, reduce_everywhere(): got = lax.ppermute(value, 'grp', CORE_PAIRS)  9.64 us
    ppermute x3, starting transfers between devices, shards(): lax.ppermute(extra, 'tile', y_to_ends(step))  8.07 us
    ppermute x1, waiting for transfers between devices, shards(): lax.ppermute(last_part, 'tile', z_shift(2))  6.35 us
  transfers between devices with their start and end apart: 34, of which 17 were waited for; matrix products, arithmetic and copies ran while one was open for 5% of the time, Pallas kernels for 7%

commit v1 on v0

--- a/solution.py
+++ b/solution.py
@@ -174,9 +174,13 @@
 def local_kernel(info, x0, x1, top, bottom, x3, local, local_row, own):
     for (r, skip, rows), x in zip(PIECES, (x0, x1, top, bottom, x3)):
         store_kept(keep_rows(info, OWN, r, skip, rows, 128), x, own, r * ROWS + skip)
-    for c in range(CHUNKS):
-        here = pl.ds(c * CHUNK, CHUNK)
+
+    def step(c, carry):
+        here = pl.ds(pl.multiple_of(c * CHUNK, CHUNK), CHUNK)
         local[here, :] = dot_rows(own[:, here], own[...])
+        return carry
+
+    lax.fori_loop(0, CHUNKS, step, 0)
     local_row[...] = dot(jnp.ones((8, PLANE), BF), own[...])
 
 
@@ -184,9 +188,13 @@
     start = 0
     for f in (f0, f1, top, bottom, f3):
         rows = f.shape[0]
-        for c in range(DIN // CHUNK):
-            here = pl.ds(c * CHUNK, CHUNK)
+
+        def step(c, carry, f=f, start=start, rows=rows):
+            here = pl.ds(pl.multiple_of(c * CHUNK, CHUNK), CHUNK)
             out[here, start : start + rows] = f[:, here].astype(F32).T.astype(BF)
+            return carry
+
+        lax.fori_loop(0, DIN // CHUNK, step, 0)
         start += rows
 
 
@@ -274,9 +282,9 @@
     mean_col[...] = mean_row[...].T
     def each(body, start=0):
         def step(c, carry):
-            return body(pl.ds(pl.multiple_of(c * CHUNK, CHUNK), CHUNK), carry)
-
-        return lax.fori_loop(0, CHUNKS, step, start)
+            return body(pl.ds(pl.multiple_of(c * 384, 384), 384), carry)
+
+        return lax.fori_loop(0, D // 384, step, start)
 
     def center(here, squares):
         value = covar[here, :] * inverse - mean_col[here, 0:1] * mean_row[0:1, :]
@@ -353,10 +361,14 @@
     core = info[PLACE + 4]
     half = DIN // 2
     for place, out in ((1 - core, sent), (core, mine)):
-        for c in range(half // CHUNK):
+
+        def step(c, carry, place=place, out=out):
             here = pl.ds(pl.multiple_of(place * half + c * CHUNK, CHUNK), CHUNK)
             value = dot(flipped[here, :], plane[...])
-            out[c * CHUNK : (c + 1) * CHUNK, :] = value.astype(out.dtype)
+            out[pl.ds(pl.multiple_of(c * CHUNK, CHUNK), CHUNK), :] = value.astype(out.dtype)
+            return carry
+
+        lax.fori_loop(0, half // CHUNK, step, 0)
 
 
 def split_kernel(place, mine, *refs):
@@ -398,8 +410,14 @@
 
 def final_kernel(core, own, other, out):
     rows = own.shape[0]
-    out[pl.ds(pl.multiple_of(core[0] * rows, rows), rows), :] = own[...].astype(F32)
-    out[pl.ds(pl.multiple_of((1 - core[0]) * rows, rows), rows), :] = other[...].astype(F32)
+
+    def step(c, carry):
+        here = pl.ds(pl.multiple_of(c * 128, 128), 128)
+        for place, value in ((core[0], own), (1 - core[0], other)):
+            out[pl.ds(pl.multiple_of(place * rows + c * 128, 128), 128), :] = value[here, :].astype(F32)
+        return carry
+
+    lax.fori_loop(0, rows // 128, step, 0)
 
 
 def three(values, axis, shift):

time: 165 us -> 165 us (level)
  waiting for transfers between devices: 42.1 us -> 40 us
  transfers between devices with their start and end apart: 34 -> 34, of which waited for: 17 -> 15; matrix products, arithmetic and copies ran while one was open for 5% -> 5% of each run, Pallas kernels for 7% -> 8%
where the time goes in v1:
time: 165 us; the launch traced here: 164 us
  starting transfers between devices  70.1 us (42%)
  waiting for transfers between devices  40 us (24%)
  Pallas kernels  34.6 us (21%)
  local copies, waits for them, and re-layouts  11.1 us (7%)
  matrix products  7.16 us (4%)
    ppermute x12, waiting for transfers between devices, three(): lax.ppermute(v, axis, shift(step))  18.6 us
    pallas_call x1, Pallas kernels, shards(): call(pool_kernel, [struct((rows, D), BF) for _, _, rows in PIECES], [SMEM...  14.4 us
    ppermute x12, starting transfers between devices, three(): lax.ppermute(v, axis, shift(step))  13.9 us
    unnamed x56, local copies, waits for them, and re-layouts  10.1 us
    all_to_all x1, starting transfers between devices, shards(): grads = lax.all_to_all(outgoing, 'tile', 0, 0, tiled=True).reshape(D, D)  9.84 us
    ppermute x1, starting transfers between devices, reduce_everywhere(): got = lax.ppermute(value, 'grp', CORE_PAIRS)  9.61 us
    ppermute x3, starting transfers between devices, shards(): lax.ppermute(extra, 'tile', y_to_ends(step))  8.07 us
    ppermute x1, waiting for transfers between devices, shards(): lax.ppermute(last_part, 'tile', z_shift(2))  5.99 us
  transfers between devices with their start and end apart: 34, of which 15 were waited for; matrix products, arithmetic and copies ran while one was open for 5% of the time, Pallas kernels for 8%

profile of v1, /device:TPU:1, one launch (start us, length us, event | category | flops | bytes accessed | tf_op | source)
XLA Modules:
  0.0 164.2 jit_solution(13952522656092099276)
XLA Ops:
  0.6 2.2 %collective-permute-start = (bf16[256,1024]{1,0:T(8,128)(2,1)}, bf16[256,1024]{1,0:T(8,128)(2,1)S(1)}, u32[]{:S(2)}, u32[]{:S(2)}) collective-permute-start(bf16[256,1024]{1,0:T(8,128)(2,1)} %f0.1), channel_id=1, source_target_pairs={{0,1},{1,2},{2,3},{3,0},{4,5},{5,6},{6,7},{7,4},{8,9},{9,10},{10,1... | collective-permute-start | bytes 1572872 | tf_op jit(solution)/shard_map/ppermute | solution.py:480
  6.8 1.6 shard_map.68
  9.5 9.8 %all-to-all-start = ((bf16[32,24,768]{2,1,0:T(8,128)(2,1)}), bf16[32,24,768]{2,1,0:T(8,128)(2,1)S(1)}, u32[]{:S(2)}, u32[]{:S(2)}) async-start(bf16[32,24,768]{2,1,0:T(8,128)(2,1)} %copy-done.1), calls=%async_computation | async-start | bytes 2359296 | tf_op jit(solution)/shard_map/all_to_all | solution.py:475
  19.3 1.6 convolution_convert_fusion.3.x0
  25.6 1.6 convolution_convert_fusion.2.x1
  27.2 1.8 %convolution_convert_fusion.1.x3 = bf16[256,768]{1,0:T(8,128)(2,1)S(1)} fusion(bf16[256,1024]{1,0:T(8,128)(2,1)} %collective-permute-done.2.f3, bf16[1024,768]{1,0:T(8,128)(2,1)S(1)} %copy-done), kind=kOutput, calls=%fused_computation.1 | convolution fusion | flops 402849792 | bytes 2490368 | tf_op jit(solution)/shard_map/dot_general | solution.py:59
  29.0 5.7 %collective-permute-done.1.top = bf16[128,1024]{1,0:T(8,128)(2,1)S(1)} collective-permute-done((bf16[128,1024]{1,0:T(8,128)(2,1)S(1)}, bf16[128,1024]{1,0:T(8,128)(2,1)S(1)}, u32[]{:S(2)}, u32[]{:S(2)}) %collective-permute-start.1) | collective-permute-done | bytes 262176 | tf_op jit(solution)/shard_map/ppermute | solution.py:482
  35.5 2.9 %shard_map.71 = (bf16[688,128]{1,0:T(8,128)(2,1)}, bf16[688,128]{1,0:T(8,128)(2,1)}) custom-call(s32[21]{0:T(128)S(1)} %get-tuple-element.47.info, bf16[256,768]{1,0:T(8,128)(2,1)S(1)} %convolution_convert_fusion.3.x0, bf16[256,768]{1,0:T(8,128)(2,1)S(1)} %convolution_convert_fusion.2.x1, bf16[128,768]{1,0:T(8,128)(2,1)S(1)} %convolution_convert_fusion.5.top.xt, ...), custom_call_target="tpu_custom_call" | custom-call | flops 5000000000 | bytes 10000000 | tf_op jit(solution)/shard_map/pallas_call | solution.py:489
  38.4 1.8 %collective-permute-start.4 = (bf16[688,128]{1,0:T(8,128)(2,1)}, bf16[688,128]{1,0:T(8,128)(2,1)S(1)}, u32[]{:S(2)}, u32[]{:S(2)}) collective-permute-start(bf16[688,128]{1,0:T(8,128)(2,1)} %get-tuple-element.51), channel_id=1, source_target_pairs={{0,4},{1,5},{2,6},{3,7},{4,8},{5,9},{6,10},{7,11},{8,12},{9,13},{1... | collective-permute-start | bytes 528392 | tf_op jit(solution)/shard_map/ppermute | solution.py:508
  41.6 2.6 %collective-permute-start.5 = (bf16[688,128]{1,0:T(8,128)(2,1)}, bf16[688,128]{1,0:T(8,128)(2,1)}, u32[]{:S(2)}, u32[]{:S(2)}) collective-permute-start(bf16[688,128]{1,0:T(8,128)(2,1)} %get-tuple-element.52), channel_id=1, source_target_pairs={{0,28},{1,29},{2,30},{3,31},{4,0},{5,1},{6,2},{7,3},{8,4},{9,5},{1... | collective-permute-start | bytes 528392 | tf_op jit(solution)/shard_map/ppermute | solution.py:509
  45.1 3.1 %shard_map.69 = (f32[768,768]{1,0:T(8,128)S(1)}, f32[8,768]{1,0:T(8,128)S(1)}) custom-call(s32[21]{0:T(128)S(1)} %get-tuple-element.47.info, bf16[256,768]{1,0:T(8,128)(2,1)S(1)} %convolution_convert_fusion.3.x0, bf16[256,768]{1,0:T(8,128)(2,1)S(1)} %convolution_convert_fusion.2.x1, bf16[128,768]{1,0:T(8,128)(2,1)S(1)} %convolution_convert_fusion.5.top.xt, ...), custom_call_target="tpu_custom_call" | custom-call | flops 5000000000 | bytes 10000000 | tf_op jit(solution)/shard_map/pallas_call | solution.py:496
  51.0 6.0 %collective-permute-done.6.left_2 = bf16[688,128]{1,0:T(8,128)(2,1)} collective-permute-done((bf16[688,128]{1,0:T(8,128)(2,1)}, bf16[688,128]{1,0:T(8,128)(2,1)}, u32[]{:S(2)}, u32[]{:S(2)}) %collective-permute-start.6) | collective-permute-done | bytes 176160 | tf_op jit(solution)/shard_map/ppermute | solution.py:510
  61.3 5.5 %collective-permute-start.10 = (bf16[688,128]{1,0:T(8,128)(2,1)S(1)}, bf16[688,128]{1,0:T(8,128)(2,1)S(1)}, u32[]{:S(2)}, u32[]{:S(2)}) collective-permute-start(bf16[688,128]{1,0:T(8,128)(2,1)S(1)} %get-tuple-element.60), channel_id=1, source_target_pairs={{1,0},{0,3},{5,4},{4,7},{9,8},{8,11},{13,12},{12,15},{17,16},{16,1... | collective-permute-start | bytes 528392 | tf_op jit(solution)/shard_map/ppermute | solution.py:517
  66.8 3.1 %shard_map.74.flipped = bf16[1024,1024]{1,0:T(8,128)(2,1)S(1)} custom-call(bf16[256,1024]{1,0:T(8,128)(2,1)S(1)} %copy-done.17, bf16[256,1024]{1,0:T(8,128)(2,1)S(1)} %copy-done.14, bf16[128,1024]{1,0:T(8,128)(2,1)S(1)} %collective-permute-done.1.top, bf16[128,1024]{1,0:T(8,128)(2,1)S(1)} %collective-permute-done.3.bottom, ...), custom_call_target="tpu_custom_call" | custom-call | flops 5000000000 | bytes 10000000 | tf_op jit(solution)/shard_map/pallas_call | solution.py:503
  70.8 14.4 %shard_map.73 = (bf16[256,768]{1,0:T(8,128)(2,1)S(1)}, bf16[256,768]{1,0:T(8,128)(2,1)S(1)}, bf16[128,768]{1,0:T(8,128)(2,1)S(1)}, bf16[128,768]{1,0:T(8,128)(2,1)S(1)}, bf16[256,768]{1,0:T(8,128)(2,1)S(1)}) custom-call(s32[21]{0:T(128)S(1)} %get-tuple-element.47.info, f32[768,768]{1,0:T(8,128)S(1)} %copy-done.27, f32[8,768]{1,0:T(8,128)S(1)} %get-tuple-element.49.local_row, ...), custom_call_target="tpu_custom_call" | custom-call | flops 5000000000 | bytes 10000000 | tf_op jit(solution)/shard_map/pallas_call | solution.py:522
  85.2 3.3 %shard_map.75 = (bf16[512,768]{1,0:T(8,128)(2,1)}, bf16[512,768]{1,0:T(8,128)(2,1)S(1)}) custom-call(s32[21]{0:T(128)S(1)} %get-tuple-element.47.info, bf16[256,768]{1,0:T(8,128)(2,1)S(1)} %get-tuple-element.62.g0, bf16[256,768]{1,0:T(8,128)(2,1)S(1)} %get-tuple-element.63.g1, bf16[128,768]{1,0:T(8,128)(2,1)S(1)} %get-tuple-element.64.gt, ...), custom_call_target="tpu_custom_call" | custom-call | flops 5000000000 | bytes 10000000 | tf_op jit(solution)/shard_map/pallas_call | solution.py:530
  88.5 4.7 %collective-permute-start.11 = (bf16[512,768]{1,0:T(8,128)(2,1)}, bf16[512,768]{1,0:T(8,128)(2,1)S(1)}, u32[]{:S(2)}, u32[]{:S(2)}) collective-permute-start(bf16[512,768]{1,0:T(8,128)(2,1)} %get-tuple-element.68), channel_id=1, source_target_pairs={{0,32},{32,0},{64,96},{96,64},{128,160},{160,128},{192,224},{224,1... | collective-permute-start | bytes 2359304 | tf_op jit(solution)/shard_map/ppermute | solution.py:436
  93.2 2.7 %collective-permute-start.16 = (bf16[128,768]{1,0:T(8,128)(2,1)}, bf16[128,768]{1,0:T(8,128)(2,1)}, u32[]{:S(2)}, u32[]{:S(2)}) collective-permute-start(bf16[128,768]{1,0:T(8,128)(2,1)} %copy-done.18), channel_id=1, source_target_pairs={{0,3},{1,0},{2,1},{3,2},{4,7},{5,4},{6,5},{7,6},{8,11},{9,8},{10,9... | collective-permute-start | bytes 589832 | tf_op jit(solution)/shard_map/ppermute | solution.py:430
  101.8 3.0 %collective-permute-done.12.refs_0_ = bf16[128,768]{1,0:T(8,128)(2,1)S(1)} collective-permute-done((bf16[128,768]{1,0:T(8,128)(2,1)}, bf16[128,768]{1,0:T(8,128)(2,1)S(1)}, u32[]{:S(2)}, u32[]{:S(2)}) %collective-permute-start.12) | collective-permute-done | bytes 196640 | tf_op jit(solution)/shard_map/ppermute | solution.py:424
  104.8 5.2 %collective-permute-done.14.refs_2_ = bf16[128,768]{1,0:T(8,128)(2,1)S(1)} collective-permute-done((bf16[128,768]{1,0:T(8,128)(2,1)}, bf16[128,768]{1,0:T(8,128)(2,1)S(1)}, u32[]{:S(2)}, u32[]{:S(2)}) %collective-permute-start.14) | collective-permute-done | bytes 196640 | tf_op jit(solution)/shard_map/ppermute | solution.py:424
  111.1 2.7 %collective-permute-start.18 = (bf16[32,768]{1,0:T(8,128)(2,1)S(1)}, bf16[32,768]{1,0:T(8,128)(2,1)S(1)}, u32[]{:S(2)}, u32[]{:S(2)}) collective-permute-start(bf16[32,768]{1,0:T(8,128)(2,1)S(1)} %get-tuple-element.78), channel_id=1, source_target_pairs={{0,3},{1,0},{2,1},{3,2},{4,7},{5,4},{6,5},{7,6},{8,11},{9,8},{10,9... | collective-permute-start | bytes 147464 | tf_op jit(solution)/shard_map/ppermute | solution.py:424
  119.8 2.6 %collective-permute-start.20 = (bf16[32,768]{1,0:T(8,128)(2,1)S(1)}, bf16[32,768]{1,0:T(8,128)(2,1)S(1)}, u32[]{:S(2)}, u32[]{:S(2)}) collective-permute-start(bf16[32,768]{1,0:T(8,128)(2,1)S(1)} %shard_map.79.own), channel_id=1, source_target_pairs={{0,4},{1,5},{2,6},{3,7},{4,0},{5,1},{6,2},{7,3},{8,12},{9,13},{10,... | collective-permute-start | bytes 147464 | tf_op jit(solution)/shard_map/ppermute | solution.py:446
  122.3 2.1 %collective-permute-start.21 = (bf16[32,768]{1,0:T(8,128)(2,1)S(1)}, bf16[32,768]{1,0:T(8,128)(2,1)S(1)}, u32[]{:S(2)}, u32[]{:S(2)}) collective-permute-start(bf16[32,768]{1,0:T(8,128)(2,1)S(1)} %shard_map.79.own), channel_id=1, source_target_pairs={{0,8},{1,9},{2,10},{3,11},{4,12},{5,13},{6,14},{7,15},{8,0},{9,1},... | collective-permute-start | bytes 147464 | tf_op jit(solution)/shard_map/ppermute | solution.py:446
  126.2 3.0 %collective-permute-done.22.c = bf16[32,768]{1,0:T(8,128)(2,1)S(1)} collective-permute-done((bf16[32,768]{1,0:T(8,128)(2,1)S(1)}, bf16[32,768]{1,0:T(8,128)(2,1)S(1)}, u32[]{:S(2)}, u32[]{:S(2)}) %collective-permute-start.22) | collective-permute-done | bytes 49184 | tf_op jit(solution)/shard_map/ppermute | solution.py:446
  129.9 4.7 %collective-permute-done.23.other = bf16[32,768]{1,0:T(8,128)(2,1)S(1)} collective-permute-done((bf16[32,768]{1,0:T(8,128)(2,1)S(1)}, bf16[32,768]{1,0:T(8,128)(2,1)S(1)}, u32[]{:S(2)}, u32[]{:S(2)}) %collective-permute-start.23) | collective-permute-done | bytes 49184 | tf_op jit(solution)/shard_map/ppermute | solution.py:448
  135.1 2.4 %collective-permute-start.27 = (bf16[32,768]{1,0:T(8,128)(2,1)S(1)}, bf16[32,768]{1,0:T(8,128)(2,1)S(1)}, u32[]{:S(2)}, u32[]{:S(2)}) collective-permute-start(bf16[32,768]{1,0:T(8,128)(2,1)S(1)} %shard_map.81.own), channel_id=1, source_target_pairs={{0,3},{1,0},{2,1},{3,2},{4,7},{5,4},{6,5},{7,6},{8,11},{9,8},{10,9... | collective-permute-start | bytes 147464 | tf_op jit(solution)/shard_map/ppermute | solution.py:424
  138.9 3.0 %collective-permute-done.28.c = bf16[32,768]{1,0:T(8,128)(2,1)S(1)} collective-permute-done((bf16[32,768]{1,0:T(8,128)(2,1)S(1)}, bf16[32,768]{1,0:T(8,128)(2,1)S(1)}, u32[]{:S(2)}, u32[]{:S(2)}) %collective-permute-start.28) | collective-permute-done | bytes 49184 | tf_op jit(solution)/shard_map/ppermute | solution.py:424
  142.5 2.2 %collective-permute-start.30 = (bf16[128,768]{1,0:T(8,128)(2,1)S(1)}, bf16[128,768]{1,0:T(8,128)(2,1)S(1)}, u32[]{:S(2)}, u32[]{:S(2)}) collective-permute-start(bf16[128,768]{1,0:T(8,128)(2,1)S(1)} %shard_map.82.own), channel_id=1, source_target_pairs={{0,192},{32,224},{64,0},{96,32},{128,64},{160,96},{192,128},{224,1... | collective-permute-start | bytes 589832 | tf_op jit(solution)/shard_map/ppermute | solution.py:424
  144.7 3.1 %collective-permute-done.29.a = bf16[128,768]{1,0:T(8,128)(2,1)S(1)} collective-permute-done((bf16[128,768]{1,0:T(8,128)(2,1)S(1)}, bf16[128,768]{1,0:T(8,128)(2,1)S(1)}, u32[]{:S(2)}, u32[]{:S(2)}) %collective-permute-start.29) | collective-permute-done | bytes 196640 | tf_op jit(solution)/shard_map/ppermute | solution.py:424
  147.7 1.7 %collective-permute-done.30.b = bf16[128,768]{1,0:T(8,128)(2,1)S(1)} collective-permute-done((bf16[128,768]{1,0:T(8,128)(2,1)S(1)}, bf16[128,768]{1,0:T(8,128)(2,1)S(1)}, u32[]{:S(2)}, u32[]{:S(2)}) %collective-permute-start.30) | collective-permute-done | bytes 196640 | tf_op jit(solution)/shard_map/ppermute | solution.py:424
  150.8 9.6 %collective-permute-start.32 = (bf16[512,768]{1,0:T(8,128)(2,1)S(1)}, bf16[512,768]{1,0:T(8,128)(2,1)S(1)}, u32[]{:S(2)}, u32[]{:S(2)}) collective-permute-start(bf16[512,768]{1,0:T(8,128)(2,1)S(1)} %shard_map.83.own), channel_id=1, source_target_pairs={{0,32},{32,0},{64,96},{96,64},{128,160},{160,128},{192,224},{224,1... | collective-permute-start | bytes 2359304 | tf_op jit(solution)/shard_map/ppermute | solution.py:455
  162.3 1.9 %shard_map.84 = f32[1024,768]{1,0:T(8,128)} custom-call(s32[1]{0:T(128)} %bitcast.1.core, bf16[512,768]{1,0:T(8,128)(2,1)S(1)} %shard_map.83.own, bf16[512,768]{1,0:T(8,128)(2,1)S(1)} %collective-permute-done.32.other), custom_call_target="tpu_custom_call" | custom-call | tf_op jit(solution)/shard_map/pallas_call | solution.py:456
  (118 shorter events, 41.7 us)
Async XLA Ops:
  0.6 20.3 %collective-permute-start = (bf16[256,1024]{1,0:T(8,128)(2,1)}, bf16[256,1024]{1,0:T(8,128)(2,1)S(1)}, u32[]{:S(2)}, u32[]{:S(2)}) collective-permute-start(bf16[256,1024]{1,0:T(8,128)(2,1)} %f0.1), channel_id=1, source_target_pairs={{0,1},{1,2},{2,3},{3,0},{4,5},{5,6},{6,7},{7,4},{8,9},{9,10},{10,1... | collective-permute-start | bytes 1572872 | tf_op jit(solution)/shard_map/ppermute | solution.py:480
  2.8 20.2 %collective-permute-start.2 = (bf16[256,1024]{1,0:T(8,128)(2,1)}, bf16[256,1024]{1,0:T(8,128)(2,1)}, u32[]{:S(2)}, u32[]{:S(2)}) collective-permute-start(bf16[256,1024]{1,0:T(8,128)(2,1)} %f0.1), channel_id=1, source_target_pairs={{0,3},{1,0},{2,1},{3,2},{4,7},{5,4},{6,5},{7,6},{8,11},{9,8},{10,9... | collective-permute-start | bytes 1572872 | tf_op jit(solution)/shard_map/ppermute | solution.py:481
  9.5 40.9 %all-to-all-start = ((bf16[32,24,768]{2,1,0:T(8,128)(2,1)}), bf16[32,24,768]{2,1,0:T(8,128)(2,1)S(1)}, u32[]{:S(2)}, u32[]{:S(2)}) async-start(bf16[32,24,768]{2,1,0:T(8,128)(2,1)} %copy-done.1), calls=%async_computation | async-start | bytes 2359296 | tf_op jit(solution)/shard_map/all_to_all | solution.py:475
  21.8 12.9 %collective-permute-start.1 = (bf16[128,1024]{1,0:T(8,128)(2,1)S(1)}, bf16[128,1024]{1,0:T(8,128)(2,1)S(1)}, u32[]{:S(2)}, u32[]{:S(2)}) collective-permute-start(bf16[128,1024]{1,0:T(8,128)(2,1)S(1)} %slice.8), channel_id=1, source_target_pairs={{0,1},{1,2},{2,3},{3,0},{4,5},{5,6},{6,7},{7,4},{8,9},{9,10},{10,1... | collective-permute-start | bytes 786440 | tf_op jit(solution)/shard_map/ppermute | solution.py:482
  24.1 11.0 %collective-permute-start.3 = (bf16[128,1024]{1,0:T(8,128)(2,1)S(1)}, bf16[128,1024]{1,0:T(8,128)(2,1)S(1)}, u32[]{:S(2)}, u32[]{:S(2)}) collective-permute-start(bf16[128,1024]{1,0:T(8,128)(2,1)S(1)} %slice.9), channel_id=1, source_target_pairs={{0,3},{1,0},{2,1},{3,2},{4,7},{5,4},{6,5},{7,6},{8,11},{9,8},{10,9... | collective-permute-start | bytes 786440 | tf_op jit(solution)/shard_map/ppermute | solution.py:483
  38.4 12.7 %collective-permute-start.4 = (bf16[688,128]{1,0:T(8,128)(2,1)}, bf16[688,128]{1,0:T(8,128)(2,1)S(1)}, u32[]{:S(2)}, u32[]{:S(2)}) collective-permute-start(bf16[688,128]{1,0:T(8,128)(2,1)} %get-tuple-element.51), channel_id=1, source_target_pairs={{0,4},{1,5},{2,6},{3,7},{4,8},{5,9},{6,10},{7,11},{8,12},{9,13},{1... | collective-permute-start | bytes 528392 | tf_op jit(solution)/shard_map/ppermute | solution.py:508
  40.1 16.9 %collective-permute-start.6 = (bf16[688,128]{1,0:T(8,128)(2,1)}, bf16[688,128]{1,0:T(8,128)(2,1)}, u32[]{:S(2)}, u32[]{:S(2)}) collective-permute-start(bf16[688,128]{1,0:T(8,128)(2,1)} %get-tuple-element.51), channel_id=1, source_target_pairs={{0,8},{1,9},{2,10},{3,11},{4,12},{5,13},{6,14},{7,15},{8,16},{9,17... | collective-permute-start | bytes 528392 | tf_op jit(solution)/shard_map/ppermute | solution.py:510
  41.6 9.5 %collective-permute-start.5 = (bf16[688,128]{1,0:T(8,128)(2,1)}, bf16[688,128]{1,0:T(8,128)(2,1)}, u32[]{:S(2)}, u32[]{:S(2)}) collective-permute-start(bf16[688,128]{1,0:T(8,128)(2,1)} %get-tuple-element.52), channel_id=1, source_target_pairs={{0,28},{1,29},{2,30},{3,31},{4,0},{5,1},{6,2},{7,3},{8,4},{9,5},{1... | collective-permute-start | bytes 528392 | tf_op jit(solution)/shard_map/ppermute | solution.py:509
  44.2 12.8 %collective-permute-start.7 = (bf16[688,128]{1,0:T(8,128)(2,1)}, bf16[688,128]{1,0:T(8,128)(2,1)}, u32[]{:S(2)}, u32[]{:S(2)}) collective-permute-start(bf16[688,128]{1,0:T(8,128)(2,1)} %get-tuple-element.52), channel_id=1, source_target_pairs={{0,24},{1,25},{2,26},{3,27},{4,28},{5,29},{6,30},{7,31},{8,0},{9,1... | collective-permute-start | bytes 528392 | tf_op jit(solution)/shard_map/ppermute | solution.py:511
  58.6 11.3 %collective-permute-start.8 = (bf16[688,128]{1,0:T(8,128)(2,1)S(1)}, bf16[688,128]{1,0:T(8,128)(2,1)S(1)}, u32[]{:S(2)}, u32[]{:S(2)}) collective-permute-start(bf16[688,128]{1,0:T(8,128)(2,1)S(1)} %get-tuple-element.58), channel_id=1, source_target_pairs={{3,0},{2,3},{7,4},{6,7},{11,8},{10,11},{15,12},{14,15},{19,16},{18... | collective-permute-start | bytes 528392 | tf_op jit(solution)/shard_map/ppermute | solution.py:517
  59.9 10.0 %collective-permute-start.9 = (bf16[688,128]{1,0:T(8,128)(2,1)S(1)}, bf16[688,128]{1,0:T(8,128)(2,1)S(1)}, u32[]{:S(2)}, u32[]{:S(2)}) collective-permute-start(bf16[688,128]{1,0:T(8,128)(2,1)S(1)} %get-tuple-element.59), channel_id=1, source_target_pairs={{2,0},{1,3},{6,4},{5,7},{10,8},{9,11},{14,12},{13,15},{18,16},{17,... | collective-permute-start | bytes 528392 | tf_op jit(solution)/shard_map/ppermute | solution.py:517
  61.3 9.4 %collective-permute-start.10 = (bf16[688,128]{1,0:T(8,128)(2,1)S(1)}, bf16[688,128]{1,0:T(8,128)(2,1)S(1)}, u32[]{:S(2)}, u32[]{:S(2)}) collective-permute-start(bf16[688,128]{1,0:T(8,128)(2,1)S(1)} %get-tuple-element.60), channel_id=1, source_target_pairs={{1,0},{0,3},{5,4},{4,7},{9,8},{8,11},{13,12},{12,15},{17,16},{16,1... | collective-permute-start | bytes 528392 | tf_op jit(solution)/shard_map/ppermute | solution.py:517
  88.5 7.4 %collective-permute-start.11 = (bf16[512,768]{1,0:T(8,128)(2,1)}, bf16[512,768]{1,0:T(8,128)(2,1)S(1)}, u32[]{:S(2)}, u32[]{:S(2)}) collective-permute-start(bf16[512,768]{1,0:T(8,128)(2,1)} %get-tuple-element.68), channel_id=1, source_target_pairs={{0,32},{32,0},{64,96},{96,64},{128,160},{160,128},{192,224},{224,1... | collective-permute-start | bytes 2359304 | tf_op jit(solution)/shard_map/ppermute | solution.py:436
  93.2 8.6 %collective-permute-start.15 = (bf16[128,768]{1,0:T(8,128)(2,1)}, bf16[128,768]{1,0:T(8,128)(2,1)}, u32[]{:S(2)}, u32[]{:S(2)}) collective-permute-start(bf16[128,768]{1,0:T(8,128)(2,1)} %copy-done.19), channel_id=1, source_target_pairs={{0,1},{1,2},{2,3},{3,0},{4,5},{5,6},{6,7},{7,4},{8,9},{9,10},{10,1... | collective-permute-start | bytes 589832 | tf_op jit(solution)/shard_map/ppermute | solution.py:429
  93.2 8.6 %collective-permute-start.16 = (bf16[128,768]{1,0:T(8,128)(2,1)}, bf16[128,768]{1,0:T(8,128)(2,1)}, u32[]{:S(2)}, u32[]{:S(2)}) collective-permute-start(bf16[128,768]{1,0:T(8,128)(2,1)} %copy-done.18), channel_id=1, source_target_pairs={{0,3},{1,0},{2,1},{3,2},{4,7},{5,4},{6,5},{7,6},{8,11},{9,8},{10,9... | collective-permute-start | bytes 589832 | tf_op jit(solution)/shard_map/ppermute | solution.py:430
  97.5 7.2 %collective-permute-start.12 = (bf16[128,768]{1,0:T(8,128)(2,1)}, bf16[128,768]{1,0:T(8,128)(2,1)S(1)}, u32[]{:S(2)}, u32[]{:S(2)}) collective-permute-start(bf16[128,768]{1,0:T(8,128)(2,1)} %get-tuple-element.70), channel_id=1, source_target_pairs={{0,64},{32,96},{64,128},{96,160},{128,192},{160,224},{192,0},{224,... | collective-permute-start | bytes 589832 | tf_op jit(solution)/shard_map/ppermute | solution.py:424
  98.7 6.0 %collective-permute-start.13 = (bf16[128,768]{1,0:T(8,128)(2,1)}, bf16[128,768]{1,0:T(8,128)(2,1)S(1)}, u32[]{:S(2)}, u32[]{:S(2)}) collective-permute-start(bf16[128,768]{1,0:T(8,128)(2,1)} %get-tuple-element.71), channel_id=1, source_target_pairs={{0,192},{32,224},{64,0},{96,32},{128,64},{160,96},{192,128},{224,1... | collective-permute-start | bytes 589832 | tf_op jit(solution)/shard_map/ppermute | solution.py:424
  100.2 9.8 %collective-permute-start.14 = (bf16[128,768]{1,0:T(8,128)(2,1)}, bf16[128,768]{1,0:T(8,128)(2,1)S(1)}, u32[]{:S(2)}, u32[]{:S(2)}) collective-permute-start(bf16[128,768]{1,0:T(8,128)(2,1)} %get-tuple-element.72), channel_id=1, source_target_pairs={{0,128},{32,160},{64,192},{96,224},{128,0},{160,32},{192,64},{224,... | collective-permute-start | bytes 589832 | tf_op jit(solution)/shard_map/ppermute | solution.py:424
  111.1 6.5 %collective-permute-start.17 = (bf16[32,768]{1,0:T(8,128)(2,1)S(1)}, bf16[32,768]{1,0:T(8,128)(2,1)S(1)}, u32[]{:S(2)}, u32[]{:S(2)}) collective-permute-start(bf16[32,768]{1,0:T(8,128)(2,1)S(1)} %get-tuple-element.77), channel_id=1, source_target_pairs={{0,1},{1,2},{2,3},{3,0},{4,5},{5,6},{6,7},{7,4},{8,9},{9,10},{10,1... | collective-permute-start | bytes 147464 | tf_op jit(solution)/shard_map/ppermute | solution.py:424
  111.1 6.4 %collective-permute-start.18 = (bf16[32,768]{1,0:T(8,128)(2,1)S(1)}, bf16[32,768]{1,0:T(8,128)(2,1)S(1)}, u32[]{:S(2)}, u32[]{:S(2)}) collective-permute-start(bf16[32,768]{1,0:T(8,128)(2,1)S(1)} %get-tuple-element.78), channel_id=1, source_target_pairs={{0,3},{1,0},{2,1},{3,2},{4,7},{5,4},{6,5},{7,6},{8,11},{9,8},{10,9... | collective-permute-start | bytes 147464 | tf_op jit(solution)/shard_map/ppermute | solution.py:424
  113.8 4.4 %collective-permute-start.19 = (bf16[32,768]{1,0:T(8,128)(2,1)S(1)}, bf16[32,768]{1,0:T(8,128)(2,1)S(1)}, u32[]{:S(2)}, u32[]{:S(2)}) collective-permute-start(bf16[32,768]{1,0:T(8,128)(2,1)S(1)} %get-tuple-element.79), channel_id=1, source_target_pairs={{0,2},{1,3},{2,0},{3,1},{4,6},{5,7},{6,4},{7,5},{8,10},{9,11},{10,... | collective-permute-start | bytes 147464 | tf_op jit(solution)/shard_map/ppermute | solution.py:424
  118.3 16.4 %collective-permute-start.24 = (bf16[256,768]{1,0:T(8,128)(2,1)S(1)}, bf16[256,768]{1,0:T(8,128)(2,1)S(1)}, u32[]{:S(2)}, u32[]{:S(2)}) collective-permute-start(bf16[256,768]{1,0:T(8,128)(2,1)S(1)} %get-tuple-element.87), channel_id=1, source_target_pairs={{0,3},{1,0},{2,1},{3,2},{4,7},{5,4},{6,5},{7,6},{8,11},{9,8},{10,9... | collective-permute-start | bytes 1179656 | tf_op jit(solution)/shard_map/ppermute | solution.py:445
  119.2 15.5 %collective-permute-start.25 = (bf16[256,768]{1,0:T(8,128)(2,1)S(1)}, bf16[256,768]{1,0:T(8,128)(2,1)S(1)}, u32[]{:S(2)}, u32[]{:S(2)}) collective-permute-start(bf16[256,768]{1,0:T(8,128)(2,1)S(1)} %get-tuple-element.88), channel_id=1, source_target_pairs={{0,1},{1,2},{2,3},{3,0},{4,5},{5,6},{6,7},{7,4},{8,9},{9,10},{10,1... | collective-permute-start | bytes 1179656 | tf_op jit(solution)/shard_map/ppermute | solution.py:445
  119.8 5.7 %collective-permute-start.20 = (bf16[32,768]{1,0:T(8,128)(2,1)S(1)}, bf16[32,768]{1,0:T(8,128)(2,1)S(1)}, u32[]{:S(2)}, u32[]{:S(2)}) collective-permute-start(bf16[32,768]{1,0:T(8,128)(2,1)S(1)} %shard_map.79.own), channel_id=1, source_target_pairs={{0,4},{1,5},{2,6},{3,7},{4,0},{5,1},{6,2},{7,3},{8,12},{9,13},{10,... | collective-permute-start | bytes 147464 | tf_op jit(solution)/shard_map/ppermute | solution.py:446
  124.4 4.7 %collective-permute-start.22 = (bf16[32,768]{1,0:T(8,128)(2,1)S(1)}, bf16[32,768]{1,0:T(8,128)(2,1)S(1)}, u32[]{:S(2)}, u32[]{:S(2)}) collective-permute-start(bf16[32,768]{1,0:T(8,128)(2,1)S(1)} %shard_map.79.own), channel_id=1, source_target_pairs={{0,12},{1,13},{2,14},{3,15},{4,8},{5,9},{6,10},{7,11},{8,4},{9,5},... | collective-permute-start | bytes 147464 | tf_op jit(solution)/shard_map/ppermute | solution.py:446
  129.2 5.5 %collective-permute-start.23 = (bf16[32,768]{1,0:T(8,128)(2,1)S(1)}, bf16[32,768]{1,0:T(8,128)(2,1)S(1)}, u32[]{:S(2)}, u32[]{:S(2)}) collective-permute-start(bf16[32,768]{1,0:T(8,128)(2,1)S(1)} %shard_map.80.own), channel_id=1, source_target_pairs={{0,24},{1,25},{2,26},{3,27},{4,28},{5,29},{6,30},{7,31},{8,16},{9,... | collective-permute-start | bytes 147464 | tf_op jit(solution)/shard_map/ppermute | solution.py:448
  134.7 4.2 %collective-permute-start.26 = (bf16[32,768]{1,0:T(8,128)(2,1)S(1)}, bf16[32,768]{1,0:T(8,128)(2,1)S(1)}, u32[]{:S(2)}, u32[]{:S(2)}) collective-permute-start(bf16[32,768]{1,0:T(8,128)(2,1)S(1)} %shard_map.81.own), channel_id=1, source_target_pairs={{0,1},{1,2},{2,3},{3,0},{4,5},{5,6},{6,7},{7,4},{8,9},{9,10},{10,1... | collective-permute-start | bytes 147464 | tf_op jit(solution)/shard_map/ppermute | solution.py:424
  137.4 4.4 %collective-permute-start.28 = (bf16[32,768]{1,0:T(8,128)(2,1)S(1)}, bf16[32,768]{1,0:T(8,128)(2,1)S(1)}, u32[]{:S(2)}, u32[]{:S(2)}) collective-permute-start(bf16[32,768]{1,0:T(8,128)(2,1)S(1)} %shard_map.81.own), channel_id=1, source_target_pairs={{0,2},{1,3},{2,0},{3,1},{4,6},{5,7},{6,4},{7,5},{8,10},{9,11},{10,... | collective-permute-start | bytes 147464 | tf_op jit(solution)/shard_map/ppermute | solution.py:424
  141.9 5.8 %collective-permute-start.29 = (bf16[128,768]{1,0:T(8,128)(2,1)S(1)}, bf16[128,768]{1,0:T(8,128)(2,1)S(1)}, u32[]{:S(2)}, u32[]{:S(2)}) collective-permute-start(bf16[128,768]{1,0:T(8,128)(2,1)S(1)} %shard_map.82.own), channel_id=1, source_target_pairs={{0,64},{32,96},{64,128},{96,160},{128,192},{160,224},{192,0},{224,... | collective-permute-start | bytes 589832 | tf_op jit(solution)/shard_map/ppermute | solution.py:424
  142.5 6.9 %collective-permute-start.30 = (bf16[128,768]{1,0:T(8,128)(2,1)S(1)}, bf16[128,768]{1,0:T(8,128)(2,1)S(1)}, u32[]{:S(2)}, u32[]{:S(2)}) collective-permute-start(bf16[128,768]{1,0:T(8,128)(2,1)S(1)} %shard_map.82.own), channel_id=1, source_target_pairs={{0,192},{32,224},{64,0},{96,32},{128,64},{160,96},{192,128},{224,1... | collective-permute-start | bytes 589832 | tf_op jit(solution)/shard_map/ppermute | solution.py:424
  144.7 6.0 %collective-permute-start.31 = (bf16[128,768]{1,0:T(8,128)(2,1)S(1)}, bf16[128,768]{1,0:T(8,128)(2,1)S(1)}, u32[]{:S(2)}, u32[]{:S(2)}) collective-permute-start(bf16[128,768]{1,0:T(8,128)(2,1)S(1)} %shard_map.82.own), channel_id=1, source_target_pairs={{0,128},{32,160},{64,192},{96,224},{128,0},{160,32},{192,64},{224,... | collective-permute-start | bytes 589832 | tf_op jit(solution)/shard_map/ppermute | solution.py:424
  150.8 11.5 %collective-permute-start.32 = (bf16[512,768]{1,0:T(8,128)(2,1)S(1)}, bf16[512,768]{1,0:T(8,128)(2,1)S(1)}, u32[]{:S(2)}, u32[]{:S(2)}) collective-permute-start(bf16[512,768]{1,0:T(8,128)(2,1)S(1)} %shard_map.83.own), channel_id=1, source_target_pairs={{0,32},{32,0},{64,96},{96,64},{128,160},{160,128},{192,224},{224,1... | collective-permute-start | bytes 2359304 | tf_op jit(solution)/shard_map/ppermute | solution.py:455
  (30 other events, 192.3 us)
